TPU v7x, 256 devices: a whole 4x4x8 slice. The times are simulated.
256 devices in a mesh: tm: 32 (over z, x), sx: 2 (over core), sy: 4 (over y).
Axes of the slice: x: 4, y: 4, z: 8, core: 2. Of those that a mesh axis runs over, the one named last changes fastest.
Arguments:
- adjoint_guess: float32 [256, 2, 64, 2048], P('tm', None, 'sx', 'sy'), may hold values from -6 to 6
- sources: float32 [256, 2, 64, 2048], P('tm', None, 'sx', 'sy'), may hold values from -2 to 2
- velocities: bfloat16 [256, 2, 64, 2048], P('tm', None, 'sx', 'sy'), may hold values from -0.29882812 to 0.29882812
- c_points: int32 [32], replicated, may hold values from 0 to 7
Outputs:
- adjoint_iterate: float32 [256, 2, 64, 2048], P('tm', None, 'sx', 'sy')
All inputs are finite; a program needn't handle non-finite values.
Results may differ from a plain program's by a relative error of at most 0.0003.
Values may be sent and summed in bfloat16 or wider, within the bound.
A program may use at most 64 MiB of HBM per device.

v0:
```python
import jax
import jax.numpy as jnp
from jax import lax
from jax.sharding import PartitionSpec as P

VISCOSITY = 0.5
TIME_STEP = 1.0


def with_halo(array, sides, width):
    for axis, dim in sides:
        devices, length = (lax.axis_size(axis), array.shape[dim])
        up = [(i, (i + 1) % devices) for i in range(devices - 1)]
        down = [(j, i) for i, j in up]
        last = lax.slice_in_dim(array, length - width, length, axis=dim)
        first = lax.slice_in_dim(array, 0, width, axis=dim)
        before = lax.ppermute(last, axis, up)
        after = lax.ppermute(first, axis, down)
        array = jnp.concatenate([before, array, after], axis=dim)
    return array


def from_behind(block, axis, distance):
    devices = range(lax.axis_size(axis))
    route = [(i - distance, i) for i in devices if i - distance in devices]
    return lax.ppermute(block, axis, route)


def flow_terms(velocity):
    u_part = velocity[..., 0, :, :]
    w_part = velocity[..., 1, :, :]
    return (
        u_part[..., 1:-1, 1:-1],
        w_part[..., 1:-1, 1:-1],
        (u_part[..., 2:, 1:-1] - u_part[..., :-2, 1:-1]) * 0.5,
        (u_part[..., 1:-1, 2:] - u_part[..., 1:-1, :-2]) * 0.5,
        (w_part[..., 2:, 1:-1] - w_part[..., :-2, 1:-1]) * 0.5,
        (w_part[..., 1:-1, 2:] - w_part[..., 1:-1, :-2]) * 0.5,
    )


def propagate(padded, terms, step_size):
    centre = padded[..., 1:-1, 1:-1]
    north = padded[..., 2:, 1:-1]
    south = padded[..., :-2, 1:-1]
    east = padded[..., 1:-1, 2:]
    west = padded[..., 1:-1, :-2]
    neighbours = north + south + east + west
    along_x = (north - south) * 0.5
    along_y = (east - west) * 0.5
    u_field, w_field, ux_field, uy_field, wx_field, wy_field = terms
    advect = u_field[..., None, :, :] * along_x + w_field[..., None, :, :] * along_y
    first = centre[..., 0, :, :]
    second = centre[..., 1, :, :]
    couple = jnp.stack(
        [ux_field * first + wx_field * second, uy_field * first + wy_field * second], axis=-3
    )
    return (centre + step_size * (VISCOSITY * neighbours + advect - couple)) / (
        1.0 + 4.0 * VISCOSITY * step_size
    )


def pick(array, index):
    return lax.dynamic_index_in_dim(array, index, 0, keepdims=False)


def shards(adjoint_guess, sources, velocities, c_points):
    steps = adjoint_guess.shape[0]
    rows = adjoint_guess.shape[2]
    columns = adjoint_guess.shape[3]
    groups = lax.axis_size("tm")
    mine = lax.axis_index("tm")
    c_here = pick(c_points, mine)
    c_next = jnp.where(mine + 1 < groups, pick(c_points, jnp.minimum(mine + 1, groups - 1)), 0)
    vel_wide = with_halo(velocities, (("sx", 2), ("sy", 3)), 1)

    def advance(field, step):
        padded = with_halo(field, (("sx", 1), ("sy", 2)), 1)
        terms = flow_terms(vel_wide[step].astype(jnp.float32))
        return propagate(padded, terms, TIME_STEP) + sources[step]

    relaxed = adjoint_guess
    field = pick(adjoint_guess, c_here)
    for turn in range(steps - 1):
        step = steps - 2 - turn
        field = field if turn == 0 else field
        update = advance(field, step)
        active = step < c_here
        field = jnp.where(active, update, field)
        relaxed = relaxed.at[step].set(jnp.where(active, update, relaxed[step]))
    field = from_behind(field, "tm", -1)
    residual = jnp.zeros((2, rows, columns), jnp.float32)
    for turn in range(steps):
        step = steps - 1 - turn
        field = field if turn == 0 else field
        update = advance(field, step)
        above = step > c_here
        relaxed = relaxed.at[step].set(jnp.where(above, update, relaxed[step]))
        residual = jnp.where(step == c_here, update - adjoint_guess[step], residual)
        field = jnp.where(above, update, field)
    span_here = (steps + c_next - c_here).astype(jnp.float32)
    coarse_terms = flow_terms(pick(vel_wide, c_here).astype(jnp.float32))

    def relay_round(counter, error):
        incoming = from_behind(error, "tm", -1)
        padded = with_halo(incoming, (("sx", 1), ("sy", 2)), 1)
        return propagate(padded, coarse_terms, TIME_STEP * span_here) + residual

    own_error = lax.fori_loop(0, groups, relay_round, jnp.zeros_like(residual))
    corrected = pick(adjoint_guess, c_here) + own_error
    return lax.dynamic_update_index_in_dim(relaxed, corrected, c_here, 0)


def solution(mesh):
    placed = (P("tm", None, "sx", "sy"), P("tm", None, "sx", "sy"), P("tm", None, "sx", "sy"), P())
    return jax.shard_map(
        shards, mesh=mesh, in_specs=placed, out_specs=P("tm", None, "sx", "sy"), check_vma=False
    )
```

profile of v0, /device:TPU:102, one launch (start us, length us, event | category | flops | bytes accessed | tf_op | source)
XLA Modules:
  0.0 1007.5 jit_solution(9623346422587781632)
XLA Ops:
  249.5 757.3 %while.28 = (s32[]{:T(128)}, f32[2,32,512]{2,1,0:T(8,128)S(1)}, f32[]{:T(128)}, f32[32,512]{1,0:T(8,128)S(1)}, f32[32,512]{1,0:T(8,128)S(1)}, /*index=5*/f32[32,...) while((s32[]{:T(128)}, f32[2,32,512]{2,1,0:T(8,128)S(1)}, ...), condition=%wide.region_1.2_spmd.clone, body=%wide.region_0.1_spmd.clone.sunk | while | flops 950547 | bytes 2428439 | solution.py:109
  251.4 8.3 collective-permute-done
  277.2 8.3 collective-permute-done
  302.7 8.3 collective-permute-done
  375.1 8.3 collective-permute-done
  398.6 8.3 collective-permute-done
  422.0 8.3 collective-permute-done
  445.5 8.3 collective-permute-done
  469.0 8.3 collective-permute-done
  492.4 8.3 collective-permute-done
  515.9 8.3 collective-permute-done
  539.4 8.3 collective-permute-done
  562.8 8.3 collective-permute-done
  586.3 8.3 collective-permute-done
  609.8 8.3 collective-permute-done
  633.3 8.3 collective-permute-done
  656.7 8.3 collective-permute-done
  680.2 8.3 collective-permute-done
  703.7 8.3 collective-permute-done
  727.1 8.3 collective-permute-done
  750.6 8.3 collective-permute-done
  821.0 8.3 collective-permute-done
  844.5 8.3 collective-permute-done
  867.9 8.3 collective-permute-done
  (805 shorter events, 797.3 us)
Async XLA Ops:
  1.4 15.7 %collective-permute-start.10 = (bf16[8,2,1,512]{3,2,1,0:T(2,128)(2,1)S(1)}, bf16[8,2,1,512]{3,2,1,0:T(2,128)(2,1)S(1)}, u32[]{:S(2)}, u32[]{:S(2)}) collective-permute-start(bf16[8,2,1,512]{3,2,1,0:T(2,128)(2,1)S(1)} %get-tuple-element.419), channel_id=1, source_target_pairs={{4,0},{5,1},{6,2},{7,3},{12,8},{13,9},{14,10},{15,11},{20,16},{21,... | collective-permute-start | bytes 49160 | tf_op jit(solution)/shard_map/ppermute | solution.py:18
  2.7 14.4 %collective-permute-start.9 = (bf16[8,2,1,512]{3,2,1,0:T(2,128)(2,1)S(1)}, bf16[8,2,1,512]{3,2,1,0:T(2,128)(2,1)S(1)}, u32[]{:S(2)}, u32[]{:S(2)}) collective-permute-start(bf16[8,2,1,512]{3,2,1,0:T(2,128)(2,1)S(1)} %get-tuple-element.418), channel_id=1, source_target_pairs={{0,4},{1,5},{2,6},{3,7},{8,12},{9,13},{10,14},{11,15},{16,20},{17,... | collective-permute-start | bytes 49160 | tf_op jit(solution)/shard_map/ppermute | solution.py:17
  8.8 13.3 %collective-permute-start.5 = (f32[2,1,512]{2,1,0:T(1,128)S(1)}, f32[2,1,512]{2,1,0:T(1,128)S(1)}, u32[]{:S(2)}, u32[]{:S(2)}) collective-permute-start(f32[2,1,512]{2,1,0:T(1,128)S(1)} %get-tuple-element.525), channel_id=1, source_target_pairs={{4,0},{5,1},{6,2},{7,3},{12,8},{13,9},{14,10},{15,11},{20,16},{21,... | collective-permute-start | bytes 12296 | tf_op jit(solution)/shard_map/ppermute | solution.py:18
  10.1 12.0 %collective-permute-start.6 = (f32[2,1,512]{2,1,0:T(1,128)S(1)}, f32[2,1,512]{2,1,0:T(1,128)S(1)}, u32[]{:S(2)}, u32[]{:S(2)}) collective-permute-start(f32[2,1,512]{2,1,0:T(1,128)S(1)} %get-tuple-element.524), channel_id=1, source_target_pairs={{0,4},{1,5},{2,6},{3,7},{8,12},{9,13},{10,14},{11,15},{16,20},{17,... | collective-permute-start | bytes 12296 | tf_op jit(solution)/shard_map/ppermute | solution.py:17
  17.3 11.4 %collective-permute-start.11 = (bf16[8,2,34,1]{3,2,1,0:T(8,128)(2,1)S(1)}, bf16[8,2,34,1]{3,2,1,0:T(8,128)(2,1)S(1)}, u32[]{:S(2)}, u32[]{:S(2)}) collective-permute-start(bf16[8,2,34,1]{3,2,1,0:T(8,128)(2,1)S(1)} %get-tuple-element.416), channel_id=1, source_target_pairs={{0,1},{1,2},{2,3},{4,5},{5,6},{6,7},{8,9},{9,10},{10,11},{12,13},{... | collective-permute-start | bytes 3272 | tf_op jit(solution)/shard_map/ppermute | solution.py:17
  115.6 10.5 %collective-permute-start.37 = (f32[2,32,512]{2,1,0:T(8,128)}, f32[2,32,512]{2,1,0:T(8,128)}, u32[]{:S(2)}, u32[]{:S(2)}) collective-permute-start(f32[2,32,512]{2,1,0:T(8,128)} %get-tuple-element.381), channel_id=1, source_target_pairs={{8,0},{16,8},{24,16},{32,24},{40,32},{48,40},{56,48},{64,56},{72,6... | collective-permute-start | bytes 393224 | tf_op jit(solution)/shard_map/ppermute | solution.py:26
  200.3 11.3 %collective-permute-start.58 = (f32[2,1,512]{2,1,0:T(1,128)S(1)}, f32[2,1,512]{2,1,0:T(1,128)S(1)}, u32[]{:S(2)}, u32[]{:S(2)}) collective-permute-start(f32[2,1,512]{2,1,0:T(1,128)S(1)} %get-tuple-element.501), channel_id=1, source_target_pairs={{4,0},{5,1},{6,2},{7,3},{12,8},{13,9},{14,10},{15,11},{20,16},{21,... | collective-permute-start | bytes 12296 | tf_op jit(solution)/shard_map/ppermute | solution.py:18
  249.5 10.2 %collective-permute-start = (f32[2,32,512]{2,1,0:T(8,128)S(1)}, f32[2,32,512]{2,1,0:T(8,128)S(1)}, u32[]{:S(2)}, u32[]{:S(2)}) collective-permute-start(f32[2,32,512]{2,1,0:T(8,128)S(1)} %broadcast_select_fusion.16), channel_id=1, source_target_pairs={{8,0},{16,8},{24,16},{32,24},{40,32},{48,40},{56,48},{64,56},{72,6... | collective-permute-start | bytes 393224 | tf_op jit(solution)/shard_map/while/body/eval_jaxpr/ppermute | solution.py:26
  275.3 10.2 %collective-permute-start = (f32[2,32,512]{2,1,0:T(8,128)S(1)}, f32[2,32,512]{2,1,0:T(8,128)S(1)}, u32[]{:S(2)}, u32[]{:S(2)}) collective-permute-start(f32[2,32,512]{2,1,0:T(8,128)S(1)} %broadcast_select_fusion.16), channel_id=1, source_target_pairs={{8,0},{16,8},{24,16},{32,24},{40,32},{48,40},{56,48},{64,56},{72,6... | collective-permute-start | bytes 393224 | tf_op jit(solution)/shard_map/while/body/eval_jaxpr/ppermute | solution.py:26
  300.8 10.2 %collective-permute-start = (f32[2,32,512]{2,1,0:T(8,128)S(1)}, f32[2,32,512]{2,1,0:T(8,128)S(1)}, u32[]{:S(2)}, u32[]{:S(2)}) collective-permute-start(f32[2,32,512]{2,1,0:T(8,128)S(1)} %broadcast_select_fusion.16), channel_id=1, source_target_pairs={{8,0},{16,8},{24,16},{32,24},{40,32},{48,40},{56,48},{64,56},{72,6... | collective-permute-start | bytes 393224 | tf_op jit(solution)/shard_map/while/body/eval_jaxpr/ppermute | solution.py:26
  326.2 10.2 %collective-permute-start = (f32[2,32,512]{2,1,0:T(8,128)S(1)}, f32[2,32,512]{2,1,0:T(8,128)S(1)}, u32[]{:S(2)}, u32[]{:S(2)}) collective-permute-start(f32[2,32,512]{2,1,0:T(8,128)S(1)} %broadcast_select_fusion.16), channel_id=1, source_target_pairs={{8,0},{16,8},{24,16},{32,24},{40,32},{48,40},{56,48},{64,56},{72,6... | collective-permute-start | bytes 393224 | tf_op jit(solution)/shard_map/while/body/eval_jaxpr/ppermute | solution.py:26
  373.2 10.2 %collective-permute-start = (f32[2,32,512]{2,1,0:T(8,128)S(1)}, f32[2,32,512]{2,1,0:T(8,128)S(1)}, u32[]{:S(2)}, u32[]{:S(2)}) collective-permute-start(f32[2,32,512]{2,1,0:T(8,128)S(1)} %broadcast_select_fusion.16), channel_id=1, source_target_pairs={{8,0},{16,8},{24,16},{32,24},{40,32},{48,40},{56,48},{64,56},{72,6... | collective-permute-start | bytes 393224 | tf_op jit(solution)/shard_map/while/body/eval_jaxpr/ppermute | solution.py:26
  396.6 10.2 %collective-permute-start = (f32[2,32,512]{2,1,0:T(8,128)S(1)}, f32[2,32,512]{2,1,0:T(8,128)S(1)}, u32[]{:S(2)}, u32[]{:S(2)}) collective-permute-start(f32[2,32,512]{2,1,0:T(8,128)S(1)} %broadcast_select_fusion.16), channel_id=1, source_target_pairs={{8,0},{16,8},{24,16},{32,24},{40,32},{48,40},{56,48},{64,56},{72,6... | collective-permute-start | bytes 393224 | tf_op jit(solution)/shard_map/while/body/eval_jaxpr/ppermute | solution.py:26
  420.1 10.2 %collective-permute-start = (f32[2,32,512]{2,1,0:T(8,128)S(1)}, f32[2,32,512]{2,1,0:T(8,128)S(1)}, u32[]{:S(2)}, u32[]{:S(2)}) collective-permute-start(f32[2,32,512]{2,1,0:T(8,128)S(1)} %broadcast_select_fusion.16), channel_id=1, source_target_pairs={{8,0},{16,8},{24,16},{32,24},{40,32},{48,40},{56,48},{64,56},{72,6... | collective-permute-start | bytes 393224 | tf_op jit(solution)/shard_map/while/body/eval_jaxpr/ppermute | solution.py:26
  443.6 10.2 %collective-permute-start = (f32[2,32,512]{2,1,0:T(8,128)S(1)}, f32[2,32,512]{2,1,0:T(8,128)S(1)}, u32[]{:S(2)}, u32[]{:S(2)}) collective-permute-start(f32[2,32,512]{2,1,0:T(8,128)S(1)} %broadcast_select_fusion.16), channel_id=1, source_target_pairs={{8,0},{16,8},{24,16},{32,24},{40,32},{48,40},{56,48},{64,56},{72,6... | collective-permute-start | bytes 393224 | tf_op jit(solution)/shard_map/while/body/eval_jaxpr/ppermute | solution.py:26
  467.0 10.2 %collective-permute-start = (f32[2,32,512]{2,1,0:T(8,128)S(1)}, f32[2,32,512]{2,1,0:T(8,128)S(1)}, u32[]{:S(2)}, u32[]{:S(2)}) collective-permute-start(f32[2,32,512]{2,1,0:T(8,128)S(1)} %broadcast_select_fusion.16), channel_id=1, source_target_pairs={{8,0},{16,8},{24,16},{32,24},{40,32},{48,40},{56,48},{64,56},{72,6... | collective-permute-start | bytes 393224 | tf_op jit(solution)/shard_map/while/body/eval_jaxpr/ppermute | solution.py:26
  490.5 10.2 %collective-permute-start = (f32[2,32,512]{2,1,0:T(8,128)S(1)}, f32[2,32,512]{2,1,0:T(8,128)S(1)}, u32[]{:S(2)}, u32[]{:S(2)}) collective-permute-start(f32[2,32,512]{2,1,0:T(8,128)S(1)} %broadcast_select_fusion.16), channel_id=1, source_target_pairs={{8,0},{16,8},{24,16},{32,24},{40,32},{48,40},{56,48},{64,56},{72,6... | collective-permute-start | bytes 393224 | tf_op jit(solution)/shard_map/while/body/eval_jaxpr/ppermute | solution.py:26
  514.0 10.2 %collective-permute-start = (f32[2,32,512]{2,1,0:T(8,128)S(1)}, f32[2,32,512]{2,1,0:T(8,128)S(1)}, u32[]{:S(2)}, u32[]{:S(2)}) collective-permute-start(f32[2,32,512]{2,1,0:T(8,128)S(1)} %broadcast_select_fusion.16), channel_id=1, source_target_pairs={{8,0},{16,8},{24,16},{32,24},{40,32},{48,40},{56,48},{64,56},{72,6... | collective-permute-start | bytes 393224 | tf_op jit(solution)/shard_map/while/body/eval_jaxpr/ppermute | solution.py:26
  537.5 10.2 %collective-permute-start = (f32[2,32,512]{2,1,0:T(8,128)S(1)}, f32[2,32,512]{2,1,0:T(8,128)S(1)}, u32[]{:S(2)}, u32[]{:S(2)}) collective-permute-start(f32[2,32,512]{2,1,0:T(8,128)S(1)} %broadcast_select_fusion.16), channel_id=1, source_target_pairs={{8,0},{16,8},{24,16},{32,24},{40,32},{48,40},{56,48},{64,56},{72,6... | collective-permute-start | bytes 393224 | tf_op jit(solution)/shard_map/while/body/eval_jaxpr/ppermute | solution.py:26
  560.9 10.2 %collective-permute-start = (f32[2,32,512]{2,1,0:T(8,128)S(1)}, f32[2,32,512]{2,1,0:T(8,128)S(1)}, u32[]{:S(2)}, u32[]{:S(2)}) collective-permute-start(f32[2,32,512]{2,1,0:T(8,128)S(1)} %broadcast_select_fusion.16), channel_id=1, source_target_pairs={{8,0},{16,8},{24,16},{32,24},{40,32},{48,40},{56,48},{64,56},{72,6... | collective-permute-start | bytes 393224 | tf_op jit(solution)/shard_map/while/body/eval_jaxpr/ppermute | solution.py:26
  584.4 10.2 %collective-permute-start = (f32[2,32,512]{2,1,0:T(8,128)S(1)}, f32[2,32,512]{2,1,0:T(8,128)S(1)}, u32[]{:S(2)}, u32[]{:S(2)}) collective-permute-start(f32[2,32,512]{2,1,0:T(8,128)S(1)} %broadcast_select_fusion.16), channel_id=1, source_target_pairs={{8,0},{16,8},{24,16},{32,24},{40,32},{48,40},{56,48},{64,56},{72,6... | collective-permute-start | bytes 393224 | tf_op jit(solution)/shard_map/while/body/eval_jaxpr/ppermute | solution.py:26
  607.9 10.2 %collective-permute-start = (f32[2,32,512]{2,1,0:T(8,128)S(1)}, f32[2,32,512]{2,1,0:T(8,128)S(1)}, u32[]{:S(2)}, u32[]{:S(2)}) collective-permute-start(f32[2,32,512]{2,1,0:T(8,128)S(1)} %broadcast_select_fusion.16), channel_id=1, source_target_pairs={{8,0},{16,8},{24,16},{32,24},{40,32},{48,40},{56,48},{64,56},{72,6... | collective-permute-start | bytes 393224 | tf_op jit(solution)/shard_map/while/body/eval_jaxpr/ppermute | solution.py:26
  631.3 10.2 %collective-permute-start = (f32[2,32,512]{2,1,0:T(8,128)S(1)}, f32[2,32,512]{2,1,0:T(8,128)S(1)}, u32[]{:S(2)}, u32[]{:S(2)}) collective-permute-start(f32[2,32,512]{2,1,0:T(8,128)S(1)} %broadcast_select_fusion.16), channel_id=1, source_target_pairs={{8,0},{16,8},{24,16},{32,24},{40,32},{48,40},{56,48},{64,56},{72,6... | collective-permute-start | bytes 393224 | tf_op jit(solution)/shard_map/while/body/eval_jaxpr/ppermute | solution.py:26
  654.8 10.2 %collective-permute-start = (f32[2,32,512]{2,1,0:T(8,128)S(1)}, f32[2,32,512]{2,1,0:T(8,128)S(1)}, u32[]{:S(2)}, u32[]{:S(2)}) collective-permute-start(f32[2,32,512]{2,1,0:T(8,128)S(1)} %broadcast_select_fusion.16), channel_id=1, source_target_pairs={{8,0},{16,8},{24,16},{32,24},{40,32},{48,40},{56,48},{64,56},{72,6... | collective-permute-start | bytes 393224 | tf_op jit(solution)/shard_map/while/body/eval_jaxpr/ppermute | solution.py:26
  (247 other events, 2248.6 us)
where the time goes:
time: 1010 us
  starting transfers between devices  478 us (47%)
  waiting for transfers between devices  467 us (46%)
  other arithmetic  33.3 us (3%)
  between operations  17.1 us (2%)
    ppermute x96, starting transfers between devices, with_halo(): before = lax.ppermute(last, axis, up)  289 us
    ppermute x33, waiting for transfers between devices, from_behind(): return lax.ppermute(block, axis, route)  271 us
    ppermute x96, waiting for transfers between devices, with_halo(): after = lax.ppermute(first, axis, down)  136 us
    ppermute x96, starting transfers between devices, with_halo(): after = lax.ppermute(first, axis, down)  124 us
    ppermute x33, starting transfers between devices, from_behind(): return lax.ppermute(block, axis, route)  64.2 us
    ppermute x96, waiting for transfers between devices, with_halo(): before = lax.ppermute(last, axis, up)  59.9 us
  transfers between devices with their start and end apart: 225, of which 155 were waited for; matrix products, arithmetic and copies ran while one was open for 1% of the time, Pallas kernels for 0%

commit v1 on v0

v1 whole, which is shorter than its diff:
```python
import jax
import jax.numpy as jnp
from jax import lax
from jax.experimental import pallas as pl
from jax.experimental.pallas import tpu as pltpu
from jax.sharding import PartitionSpec as P

F32 = jnp.float32
MESH = pl.DeviceIdType.MESH
STEPS = 8
ROWS = 32
COLS = 512
EDGE = 8
XROWS = ROWS + EDGE
XCOLS = COLS + 128
GROUPS = 32
TILES = 16
REACH = 16
LEVELS = 16


def iota(shape, dim):
    return lax.broadcasted_iota(jnp.int32, shape, dim)


def roll(x, shift, dim):
    return pltpu.roll(x, shift % x.shape[dim], dim)


def pack_edges(tiles, first):
    lane = iota((ROWS, 128), 1)
    packed = jnp.zeros((ROWS, 128), F32)
    for place, tile in enumerate(tiles):
        at = EDGE * place
        moved = roll(tile(), at if first else at + EDGE, 1)
        packed = jnp.where((lane >= at) & (lane < at + EDGE), moved, packed)
    return packed


def unpack_edges(right, left, place):
    lane = iota((XROWS, 128), 1)
    at = EDGE * place
    return jnp.where(lane < 64, roll(right, -at, 1), roll(left, -EDGE - at, 1))


def window(read, index):
    lane = iota((ROWS, 128), 1)
    tile, offset = divmod(32 * index - REACH, 128)

    def part(component, target):
        piece = read(component, tile % 4)
        if offset + 64 > 128:
            piece = jnp.where(lane >= offset, piece, read(component, (tile + 1) % 4))
        return roll(piece, target - offset, 1)

    return jnp.where(lane < 64, part(0, 0), part(1, 64))


def owner_of(tile):
    z = tile // 2
    return z * 4 + 2 * (tile % 2) + z % 2


def kernel(
    c_ref, guess, src, vel, out,
    srcx, velx, fld, nxt, co1, pk, pkr, fp, fpr, res, rw, vw,
    rbuf, xbuf, vbuf, vxbuf, coef, ebuf, ebox, nbr,
    s_a, r_a, s_b, r_b, s_v, r_v, s_r, r_r, r_rx, s_e, r_e, s_n, r_n,
):
    tm = lax.axis_index("tm")
    sx = lax.axis_index("sx")
    sy = lax.axis_index("sy")
    east = lax.rem(sy + 1, 4)
    west = lax.rem(sy + 3, 4)
    before = lax.rem(tm + GROUPS - 1, GROUPS)
    edge_row = pl.multiple_of((1 - sx) * (ROWS - EDGE), 8)
    edge = pl.ds(edge_row, EDGE)
    halo = pl.ds(ROWS, EDGE)
    here = c_ref[tm]
    z = tm // 4
    x = lax.rem(tm, 4)
    tile = 2 * z + x // 2
    is_owner = (sx == 0) & (lax.rem(x, 2) == lax.rem(z, 2))
    is_end = is_owner & ((tile == 0) | (tile == TILES - 1))

    def remote(src_ref, dst_ref, send, recv, device):
        return pltpu.make_async_remote_copy(
            src_ref=src_ref, dst_ref=dst_ref, send_sem=send, recv_sem=recv,
            device_id=device, device_id_type=MESH,
        )

    def arrived(ref, sem):
        pltpu.make_async_copy(ref, ref, sem).wait()

    srcx[:, :, 0:ROWS, 0:COLS] = src[...]
    velx[:, :, 0:ROWS, 0:COLS] = vel[...].astype(F32)
    fld[0, :, 0:ROWS, 0:COLS] = guess[here]
    own = pl.ds(0, COLS)
    copies = [
        remote(src.at[:, :, edge, :], srcx.at[:, :, halo, own], s_a.at[0], r_a.at[0], (tm, 1 - sx, sy)),
        remote(velx.at[:, :, edge, own], velx.at[:, :, halo, own], s_a.at[1], r_a.at[1], (tm, 1 - sx, sy)),
        remote(fld.at[0, :, edge, own], fld.at[0, :, halo, own], s_a.at[2], r_a.at[2], (tm, 1 - sx, sy)),
    ]
    for copy in copies:
        copy.start()
    for way, (first, lanes, target) in enumerate(
        ((True, slice(0, 128), west), (False, slice(COLS - 128, COLS), east))
    ):
        pairs = [(j, k) for j in range(STEPS) for k in range(2)]
        pk[way, 0] = pack_edges([lambda j=j, k=k: src[j, k, :, lanes] for j, k in pairs], first)
        pk[way, 1] = pack_edges([lambda j=j, k=k: velx[j, k, 0:ROWS, lanes] for j, k in pairs], first)
        pk[way, 2] = pack_edges([lambda k=k: fld[0, k, 0:ROWS, lanes] for k in range(2)], first)
        for copy in (
            remote(pk.at[way], pkr.at[way, :, 0:ROWS], s_a.at[3 + way], r_a.at[3 + way], (tm, sx, target)),
            remote(
                pk.at[way, :, edge], pkr.at[way, :, halo], s_a.at[5 + way], r_a.at[5 + way], (tm, 1 - sx, target)
            ),
        ):
            copy.start()
            copies.append(copy)

    def read_velocity(component, lane_tile):
        return vel[here, component, :, 128 * lane_tile : 128 * lane_tile + 128].astype(F32)

    for index in range(-1, TILES + 1):
        vw[index + 1] = window(read_velocity, index).astype(jnp.bfloat16)

    half = pl.ds(pl.multiple_of(sx * ROWS, ROWS), ROWS)

    def is_self(index):
        return (owner_of(index) == tm) & (sx == 0)

    def to_windows(source, boxes, extras, send, recv, recv_extra, act):
        def one(index, _):
            mine = is_self(index)

            @pl.when(mine)
            def _():
                if act:
                    pltpu.make_async_copy(source.at[index + 1], boxes.at[tm, half], send.at[index + 1]).start()

            @pl.when(jnp.logical_not(mine))
            def _():
                copy = remote(
                    source.at[index + 1], boxes.at[tm, half], send.at[index + 1], recv(tm), (owner_of(index), 0, sy)
                )
                copy.start() if act else copy.wait_send()

            return 0

        lax.fori_loop(0, TILES, one, 0)
        for index, target, device in ((0, west, owner_of(TILES - 1)), (TILES + 1, east, owner_of(0))):
            copy = remote(source.at[index], extras.at[tm, half], send.at[index], recv_extra(tm), (device, 0, target))
            copy.start() if act else copy.wait_send()

    def own_window(source, boxes, send):
        @pl.when(is_owner)
        def _():
            pltpu.make_async_copy(source.at[tile + 1], boxes.at[tm, half], send.at[tile + 1]).wait()

    to_windows(vw, vbuf, vxbuf, s_v, lambda g: r_v.at[g, 0], lambda g: r_v.at[g, 1], True)

    for copy in copies:
        copy.wait()
    to_right = jnp.where(sy < 3, 1.0, 0.0).astype(F32)
    to_left = jnp.where(sy > 0, 1.0, 0.0).astype(F32)
    right = [pkr[0, part] * to_right for part in range(3)]
    left = [pkr[1, part] * to_left for part in range(3)]
    for j in range(STEPS):
        for k in range(2):
            srcx[j, k, :, COLS:XCOLS] = unpack_edges(right[0], left[0], 2 * j + k)
            velx[j, k, :, COLS:XCOLS] = unpack_edges(right[1], left[1], 2 * j + k)
    for k in range(2):
        fld[0, k, :, COLS:XCOLS] = unpack_edges(right[2], left[2], k)

    lane = iota((EDGE, XCOLS), 1)
    row = iota((EDGE, XCOLS), 0)
    inside = (lane < COLS) | ((lane < COLS + 64) & (sy < 3)) | ((lane >= COLS + 64) & (sy > 0))
    third = jnp.where(inside, 1.0 / 3.0, 0.0).astype(F32)
    tiles = XROWS // EDGE
    last_own = ROWS // EDGE - 1
    north_ok = jnp.where((row == EDGE - 1) & (sx == 1), 0.0, 1.0).astype(F32)
    south_ok = jnp.where((row == 0) & (sx == 0), 0.0, 1.0).astype(F32)

    def around(parts):
        up = [roll(part, -1, 0) for part in parts]
        down = [roll(part, 1, 0) for part in parts]
        for i, part in enumerate(parts):
            north = jnp.where(row == EDGE - 1, up[(i + 1) % tiles], up[i])
            south = jnp.where(row == 0, down[i - 1], down[i])
            yield part, north, south, roll(part, -1, 1), roll(part, 1, 1)

    def coefficients(j, _):
        u = [velx[j, 0, EDGE * i : EDGE * (i + 1), :] for i in range(tiles)]
        w = [velx[j, 1, EDGE * i : EDGE * (i + 1), :] for i in range(tiles)]
        for i, ((uc, un, us, ue, uw), (wc, wn, ws, we, ww)) in enumerate(zip(around(u), around(w))):
            rows = slice(EDGE * i, EDGE * (i + 1))
            scale_n = scale_s = third
            if i == last_own:
                un, wn, scale_n = un * north_ok, wn * north_ok, third * north_ok
            if i == 0:
                us, ws, scale_s = us * south_ok, ws * south_ok, third * south_ok
            hu, hw = 0.5 * uc, 0.5 * wc
            ht = 0.5 * third
            co1[j, 0, rows] = third - ht * (un - us)
            co1[j, 1, rows] = -ht * (wn - ws)
            co1[j, 2, rows] = third - ht * (we - ww)
            co1[j, 3, rows] = -ht * (ue - uw)
            co1[j, 4, rows] = scale_n * (0.5 + hu)
            co1[j, 5, rows] = scale_s * (0.5 - hu)
            co1[j, 6, rows] = third * (0.5 + hw)
            co1[j, 7, rows] = third * (0.5 - hw)
        return 0

    lax.fori_loop(0, STEPS, coefficients, 0)

    def phi(field, slot, j):
        p = [field[slot, 0, EDGE * i : EDGE * (i + 1), :] for i in range(tiles)]
        q = [field[slot, 1, EDGE * i : EDGE * (i + 1), :] for i in range(tiles)]
        for i, ((pc, pn, ps, pe, pw), (qc, qn, qs, qe, qw)) in enumerate(zip(around(p), around(q))):
            rows = slice(EDGE * i, EDGE * (i + 1))
            a = [co1[j, n, rows] for n in range(8)]
            new_p = a[0] * pc + a[1] * qc + a[4] * pn + a[5] * ps + a[6] * pe + a[7] * pw + srcx[j, 0, rows]
            new_q = a[2] * qc + a[3] * pc + a[4] * qn + a[5] * qs + a[6] * qe + a[7] * qw + srcx[j, 1, rows]
            yield rows, i, ((0, pc, new_p), (1, qc, new_q))

    def lower(turn, _):
        j = STEPS - 2 - turn
        slot = lax.rem(turn, 2)
        active = j < here
        for rows, i, parts in phi(fld, slot, j):
            for k, old, new in parts:
                fld[1 - slot, k, rows] = jnp.where(active, new, old)
                if i <= last_own:
                    out[j, k, rows] = new[:, 0:COLS]
        return 0

    lax.fori_loop(0, STEPS - 1, lower, 0)
    out[STEPS - 1] = guess[STEPS - 1]
    done = (STEPS - 1) % 2

    relays = [
        remote(fld.at[done, :, 0:ROWS, own], nxt.at[0, :, 0:ROWS, own], s_b.at[0], r_b.at[0], (before, sx, sy)),
        remote(fld.at[done, :, edge, own], nxt.at[0, :, halo, own], s_b.at[1], r_b.at[1], (before, 1 - sx, sy)),
    ]
    for copy in relays:
        copy.start()
    for way, (first, lanes, target) in enumerate(
        ((True, slice(0, 128), west), (False, slice(COLS - 128, COLS), east))
    ):
        fp[way] = pack_edges([lambda k=k: fld[done, k, 0:ROWS, lanes] for k in range(2)], first)
        for copy in (
            remote(fp.at[way], fpr.at[way, 0:ROWS], s_b.at[2 + way], r_b.at[2 + way], (before, sx, target)),
            remote(fp.at[way, edge], fpr.at[way, halo], s_b.at[4 + way], r_b.at[4 + way], (before, 1 - sx, target)),
        ):
            copy.start()
            relays.append(copy)
    for copy in relays:
        copy.wait_recv()
    for k in range(2):
        nxt[0, k, :, COLS:XCOLS] = unpack_edges(fpr[0] * to_right, fpr[1] * to_left, k)

    @pl.when(tm == GROUPS - 1)
    def _():
        nxt[0] = jnp.zeros((2, XROWS, XCOLS), F32)

    def upper(turn, _):
        j = STEPS - 1 - turn
        slot = lax.rem(turn, 2)
        above = j > here
        coarse = j == here
        for rows, i, parts in phi(nxt, slot, j):
            for k, old, new in parts:
                nxt[1 - slot, k, rows] = jnp.where(above, new, old)
                if i <= last_own:
                    inner = new[:, 0:COLS]
                    out[j, k, rows] = jnp.where(above, inner, out[j, k, rows])
                    res[k, rows] = jnp.where(coarse, inner - guess[j, k, rows], res[k, rows])
        return 0

    res[...] = jnp.zeros((2, ROWS, COLS), F32)
    lax.fori_loop(0, STEPS, upper, 0)

    def read_residual(component, lane_tile):
        return res[component, :, 128 * lane_tile : 128 * lane_tile + 128]

    for index in range(-1, TILES + 1):
        rw[index + 1] = window(read_residual, index)
    to_windows(rw, rbuf, xbuf, s_r, lambda g: r_r.at[g], lambda g: r_rx.at[g], True)

    @pl.when(is_owner)
    def _():
        lane = iota((2 * ROWS, 128), 1)
        grid_row = iota((2 * ROWS, 128), 0)
        place = lax.rem(lane, 64)
        first = lane < 64
        from_extra = ((place < REACH) & (tile == 0)) | ((place >= 64 - REACH) & (tile == TILES - 1))
        outside = ((place < REACH) & (tile == 0) & (sy == 0)) | (
            (place >= 64 - REACH) & (tile == TILES - 1) & (sy == 3)
        )
        keep = jnp.where(outside, 0.0, 1.0).astype(F32)
        north = jnp.where(grid_row == 2 * ROWS - 1, 0.0, 1.0).astype(F32)
        south = jnp.where(grid_row == 0, 0.0, 1.0).astype(F32)
        own_window(vw, vbuf, s_v)
        own_window(rw, rbuf, s_r)

        def wait_velocity(level, _):
            pl.when(level != tm)(lambda: arrived(vbuf.at[level], r_v.at[level, 0]))
            pl.when(level == tm)(lambda: arrived(vbuf.at[level, ROWS : 2 * ROWS], r_v.at[level, 0]))
            return 0

        lax.fori_loop(0, GROUPS, wait_velocity, 0)

        @pl.when(is_end)
        def _():
            def merge(level, _):
                arrived(vxbuf.at[level], r_v.at[level, 1])
                both = jnp.where(from_extra, vxbuf[level].astype(F32), vbuf[level].astype(F32))
                vbuf[level] = both.astype(jnp.bfloat16)
                return 0

            lax.fori_loop(0, GROUPS, merge, 0)

        def coarse_coefficients(level, _):
            v = vbuf[level].astype(F32) * keep
            after = jnp.where(level + 1 < GROUPS, c_ref[jnp.minimum(level + 1, GROUPS - 1)], 0)
            span = jnp.full((2 * ROWS, 128), STEPS + after - c_ref[level], jnp.int32).astype(F32)
            inverse = keep / (1.0 + 2.0 * span)
            k = span * inverse
            swapped = roll(v, 64, 1)
            u = jnp.where(first, v, swapped)
            w = jnp.where(first, swapped, v)
            dx = 0.5 * (roll(v, -1, 0) * north - roll(v, 1, 0) * south)
            dy = 0.5 * (roll(v, -1, 1) - roll(v, 1, 1))
            coef[level, 0] = inverse - k * jnp.where(first, dx, dy)
            coef[level, 1] = -k * jnp.where(first, roll(dx, 64, 1), roll(dy, 64, 1))
            coef[level, 2] = k * (0.5 + 0.5 * u) * north
            coef[level, 3] = k * (0.5 - 0.5 * u) * south
            coef[level, 4] = k * (0.5 + 0.5 * w)
            coef[level, 5] = k * (0.5 - 0.5 * w)
            return 0

        lax.fori_loop(0, GROUPS, coarse_coefficients, 0)

        def send_error(level, act):
            for core in range(2):
                rows = pl.ds(core * ROWS, ROWS)

                def away(core=core, rows=rows):
                    copy = remote(
                        ebuf.at[level, rows], ebox.at[tile], s_e.at[level, core], r_e.at[tile], (level, core, sy)
                    )
                    copy.start() if act else copy.wait_send()

                if core == 1:
                    away()
                else:
                    pl.when(level != tm)(away)

                    @pl.when(level == tm)
                    def _():
                        if act:
                            pltpu.make_async_copy(ebuf.at[level, rows], ebox.at[tile], r_e.at[tile]).start()

        def solve(top):
            def one(turn, error):
                level = top - turn
                pl.when(level != tm)(lambda: arrived(rbuf.at[level], r_r.at[level]))
                pl.when(level == tm)(lambda: arrived(rbuf.at[level, ROWS : 2 * ROWS], r_r.at[level]))

                @pl.when(is_end)
                def _():
                    arrived(xbuf.at[level], r_rx.at[level])
                    rbuf[level] = jnp.where(from_extra, xbuf[level], rbuf[level])

                c = [coef[level, n] for n in range(6)]
                new = c[0] * error + c[1] * roll(error, 64, 1)
                new = new + (c[2] * roll(error, -1, 0) + c[3] * roll(error, 1, 0))
                new = new + (c[4] * roll(error, -1, 1) + c[5] * roll(error, 1, 1))
                new = new + rbuf[level] * keep
                ebuf[level] = new
                send_error(level, True)
                return new

            return one

        error = lax.fori_loop(0, LEVELS, solve(GROUPS - 1), jnp.zeros((2 * ROWS, 128), F32))
        middle = GROUPS - LEVELS
        right_tile = lax.rem(tile + 1, TILES)
        left_tile = lax.rem(tile + TILES - 1, TILES)
        right_sy = jnp.where(tile == TILES - 1, east, sy)
        left_sy = jnp.where(tile == 0, west, sy)
        sides = [
            remote(ebuf.at[middle], nbr.at[0], s_n.at[0], r_n.at[0], (owner_of(right_tile), 0, right_sy)),
            remote(ebuf.at[middle], nbr.at[1], s_n.at[1], r_n.at[1], (owner_of(left_tile), 0, left_sy)),
        ]
        for copy in sides:
            copy.start()
        for copy in sides:
            copy.wait_recv()
        error = jnp.where(place < REACH, roll(nbr[0], -32, 1), error)
        error = jnp.where(place >= 64 - REACH, roll(nbr[1], 32, 1), error) * keep
        lax.fori_loop(0, LEVELS, solve(middle - 1), error)
        for copy in sides:
            copy.wait_send()

        def wait_errors(level, _):
            send_error(level, False)
            return 0

        lax.fori_loop(0, GROUPS, wait_errors, 0)

    def wait_boxes(index, _):
        arrived(ebox.at[index], r_e.at[index])
        return 0

    lax.fori_loop(0, TILES, wait_boxes, 0)
    lane = iota((ROWS, 128), 1)
    for k in range(2):
        for lane_tile in range(4):
            whole = None
            for i in range(4):
                piece = roll(ebox[4 * lane_tile + i], 32 * i - REACH - 64 * k, 1)
                whole = piece if whole is None else jnp.where(lane >= 32 * i, piece, whole)
            res[k, :, 128 * lane_tile : 128 * lane_tile + 128] = whole

    def place_coarse(j, _):
        out[j] = jnp.where(j == here, guess[j] + res[...], out[j])
        return 0

    lax.fori_loop(0, STEPS, place_coarse, 0)

    for copy in relays:
        copy.wait_send()
    to_windows(vw, vbuf, vxbuf, s_v, lambda g: r_v.at[g, 0], lambda g: r_v.at[g, 1], False)
    to_windows(rw, rbuf, xbuf, s_r, lambda g: r_r.at[g], lambda g: r_rx.at[g], False)


def shards(adjoint_guess, sources, velocities, c_points):
    dma = pltpu.SemaphoreType.DMA
    vmem = pl.BlockSpec(memory_space=pltpu.VMEM)
    return pl.pallas_call(
        kernel,
        out_shape=jax.ShapeDtypeStruct(adjoint_guess.shape, F32),
        in_specs=[pl.BlockSpec(memory_space=pltpu.SMEM), vmem, vmem, vmem],
        out_specs=vmem,
        scratch_shapes=[
            pltpu.VMEM((STEPS, 2, XROWS, XCOLS), F32),
            pltpu.VMEM((STEPS, 2, XROWS, XCOLS), F32),
            pltpu.VMEM((2, 2, XROWS, XCOLS), F32),
            pltpu.VMEM((2, 2, XROWS, XCOLS), F32),
            pltpu.VMEM((STEPS, 8, XROWS, XCOLS), F32),
            pltpu.VMEM((2, 3, ROWS, 128), F32),
            pltpu.VMEM((2, 3, XROWS, 128), F32),
            pltpu.VMEM((2, ROWS, 128), F32),
            pltpu.VMEM((2, XROWS, 128), F32),
            pltpu.VMEM((2, ROWS, COLS), F32),
            pltpu.VMEM((TILES + 2, ROWS, 128), F32),
            pltpu.VMEM((TILES + 2, ROWS, 128), jnp.bfloat16),
            pltpu.VMEM((GROUPS, 2 * ROWS, 128), F32),
            pltpu.VMEM((GROUPS, 2 * ROWS, 128), F32),
            pltpu.VMEM((GROUPS, 2 * ROWS, 128), jnp.bfloat16),
            pltpu.VMEM((GROUPS, 2 * ROWS, 128), jnp.bfloat16),
            pltpu.VMEM((GROUPS, 6, 2 * ROWS, 128), F32),
            pltpu.VMEM((GROUPS, 2 * ROWS, 128), F32),
            pltpu.VMEM((TILES, ROWS, 128), F32),
            pltpu.VMEM((2, 2 * ROWS, 128), F32),
            dma((7,)), dma((7,)), dma((6,)), dma((6,)),
            dma((TILES + 2,)), dma((GROUPS, 2)),
            dma((TILES + 2,)), dma((GROUPS,)), dma((GROUPS,)),
            dma((GROUPS, 2)), dma((TILES,)), dma((2,)), dma((2,)),
        ],
        compiler_params=pltpu.CompilerParams(has_side_effects=True, vmem_limit_bytes=48 * 1024 * 1024),
    )(c_points, adjoint_guess, sources, velocities)


def solution(mesh):
    placed = (P("tm", None, "sx", "sy"), P("tm", None, "sx", "sy"), P("tm", None, "sx", "sy"), P())
    return jax.shard_map(
        shards, mesh=mesh, in_specs=placed, out_specs=P("tm", None, "sx", "sy"), check_vma=False
    )
```

time: 1010 us -> 78.3 us (0.08)
  the two profiles are of different devices: /device:TPU:102 before, /device:TPU:1 now
where the time goes in v1:
time: 78.3 us; the launch traced here: 78.1 us
  Pallas kernels  72.9 us (93%)
  local copies, waits for them, and re-layouts  5.12 us (7%)
    pallas_call x1, Pallas kernels, shards(): pl.pallas_call(kernel, out_shape=jax.ShapeDtypeStruct(adjoint_guess.shape...  72.9 us
    unnamed x9, local copies, waits for them, and re-layouts  5.12 us

profile of v1, /device:TPU:1, one launch (start us, length us, event | category | flops | bytes accessed | tf_op | source)
XLA Modules:
  0.0 78.1 jit_solution(14039179286703597201)
XLA Ops:
  0.0 0.0 copy-start
  0.0 1.2 %copy-done = f32[8,2,32,512]{3,2,1,0:T(8,128)S(1)} copy-done((f32[8,2,32,512]{3,2,1,0:T(8,128)S(1)}, f32[8,2,32,512]{3,2,1,0:T(8,128)}, u32[]{:S(2)}) %copy-start) | copy-done | bytes 1048600
  1.2 0.0 copy-start.1
  1.2 1.2 %copy-done.1 = f32[8,2,32,512]{3,2,1,0:T(8,128)S(1)} copy-done((f32[8,2,32,512]{3,2,1,0:T(8,128)S(1)}, f32[8,2,32,512]{3,2,1,0:T(8,128)}, u32[]{:S(2)}) %copy-start.1) | copy-done | bytes 1048600
  2.5 0.0 copy-start.2
  2.5 1.0 %copy-done.2 = bf16[8,2,32,512]{3,2,1,0:T(8,128)(2,1)S(1)} copy-done((bf16[8,2,32,512]{3,2,1,0:T(8,128)(2,1)S(1)}, bf16[8,2,32,512]{3,2,1,0:T(8,128)(2,1)}, u32[]{:S(2)}) %copy-start.2) | copy-done | bytes 524312
  3.5 0.0 copy-start.3
  3.5 0.7 copy-done.3
  4.1 72.9 %shard_map.46 = f32[8,2,32,512]{3,2,1,0:T(8,128)S(1)} custom-call(s32[32]{0:T(128)S(1)} %copy-done.3, f32[8,2,32,512]{3,2,1,0:T(8,128)S(1)} %copy-done, f32[8,2,32,512]{3,2,1,0:T(8,128)S(1)} %copy-done.1, bf16[8,2,32,512]{3,2,1,0:T(8,128)(2,1)S(1)} %copy-done.2), custom_call_target="tpu_custom_call" | custom-call | tf_op jit(solution)/shard_map/pallas_call | solution.py:442
  77.1 1.0 %copy.6 = f32[8,2,32,512]{3,2,1,0:T(8,128)} copy(f32[8,2,32,512]{3,2,1,0:T(8,128)S(1)} %shard_map.46) | data formatting | bytes 2097152
Async XLA Ops:
  0.0 1.2 %copy-start = (f32[8,2,32,512]{3,2,1,0:T(8,128)S(1)}, f32[8,2,32,512]{3,2,1,0:T(8,128)}, u32[]{:S(2)}) copy-start(f32[8,2,32,512]{3,2,1,0:T(8,128)} %guess.1) | copy-start | bytes 3145732
  1.2 1.2 %copy-start.1 = (f32[8,2,32,512]{3,2,1,0:T(8,128)S(1)}, f32[8,2,32,512]{3,2,1,0:T(8,128)}, u32[]{:S(2)}) copy-start(f32[8,2,32,512]{3,2,1,0:T(8,128)} %src.1) | copy-start | bytes 3145732
  2.5 1.0 %copy-start.2 = (bf16[8,2,32,512]{3,2,1,0:T(8,128)(2,1)S(1)}, bf16[8,2,32,512]{3,2,1,0:T(8,128)(2,1)}, u32[]{:S(2)}) copy-start(bf16[8,2,32,512]{3,2,1,0:T(8,128)(2,1)} %vel.1) | copy-start | bytes 1572868
  3.5 0.7 copy-start.3

commit v2 on v1

v2 whole, which is shorter than its diff:
```python
import jax
import jax.numpy as jnp
from jax import lax
from jax.experimental import pallas as pl
from jax.experimental.pallas import tpu as pltpu
from jax.sharding import PartitionSpec as P

F32 = jnp.float32
MESH = pl.DeviceIdType.MESH
STEPS = 8
ROWS = 32
COLS = 512
EDGE = 8
XROWS = ROWS + EDGE
XCOLS = COLS + 128
GROUPS = 32
TILES = 16
REACH = 16
BATCH = 4
LEVELS = 16


def iota(shape, dim):
    return lax.broadcasted_iota(jnp.int32, shape, dim)


def roll(x, shift, dim):
    return pltpu.roll(x, shift % x.shape[dim], dim)


def pack_edges(tiles, first):
    lane = iota((ROWS, 128), 1)
    packed = jnp.zeros((ROWS, 128), F32)
    for place, tile in enumerate(tiles):
        at = EDGE * place
        moved = roll(tile(), at if first else at + EDGE, 1)
        packed = jnp.where((lane >= at) & (lane < at + EDGE), moved, packed)
    return packed


def unpack_edges(right, left, place):
    lane = iota((XROWS, 128), 1)
    at = EDGE * place
    return jnp.where(lane < 64, roll(right, -at, 1), roll(left, -EDGE - at, 1))


def window(read, index):
    lane = iota((ROWS, 128), 1)
    tile, offset = divmod(32 * index - REACH, 128)

    def part(component, target):
        piece = read(component, tile % 4)
        if offset + 64 > 128:
            piece = jnp.where(lane >= offset, piece, read(component, (tile + 1) % 4))
        return roll(piece, target - offset, 1)

    return jnp.where(lane < 64, part(0, 0), part(1, 64))


def fold(part, step):
    lane = lax.rem(iota((EDGE, 128), 1), 64)
    at = 0 if step > 0 else 48
    folded = part[0:EDGE]
    for i in range(1, ROWS // EDGE):
        moved = roll(part[EDGE * i : EDGE * (i + 1)], step * i, 1)
        folded = jnp.where((lane >= at + step * i) & (lane < at + step * i + REACH), moved, folded)
    return folded


def owner_of(tile):
    z = tile // 2
    return z * 4 + 2 * (tile % 2) + z % 2


def kernel(
    c_hbm, guess_hbm, src_hbm, vel_hbm, out,
    c_ref, guess, vel, srcx, velx, fld, nxt, co1, pk, pkr, fp, fpr, res, upd, rw, rf, vw, vf,
    rbuf, xbuf, vbuf, vxbuf, coef, ebuf, ebox, mine, nbr,
    s_a, r_a, s_b, r_b, s_v, r_v, s_r, r_r, r_rx, s_e, r_e, s_n, r_n, s_i, known,
):
    tm = lax.axis_index("tm")
    sx = lax.axis_index("sx")
    sy = lax.axis_index("sy")
    east = lax.rem(sy + 1, 4)
    west = lax.rem(sy + 3, 4)
    before = lax.rem(tm + GROUPS - 1, GROUPS)
    edge_row = pl.multiple_of((1 - sx) * (ROWS - EDGE), 8)
    edge = pl.ds(edge_row, EDGE)
    halo = pl.ds(ROWS, EDGE)
    z = tm // 4
    x = lax.rem(tm, 4)
    tile = 2 * z + x // 2
    is_owner = (sx == 0) & (lax.rem(x, 2) == lax.rem(z, 2))
    is_end = is_owner & ((tile == 0) | (tile == TILES - 1))

    def remote(src_ref, dst_ref, send, recv, device):
        return pltpu.make_async_remote_copy(
            src_ref=src_ref, dst_ref=dst_ref, send_sem=send, recv_sem=recv,
            device_id=device, device_id_type=MESH,
        )

    def arrived(ref, sem):
        pltpu.make_async_copy(ref, ref, sem).wait()

    barrier = pltpu.get_barrier_semaphore()

    def greet(*device):
        pl.semaphore_signal(barrier, inc=1, device_id=device, device_id_type=MESH)

    fetch = [
        pltpu.make_async_copy(c_hbm, c_ref, s_i.at[0]),
        pltpu.make_async_copy(vel_hbm, vel, s_i.at[1]),
        pltpu.make_async_copy(src_hbm, srcx.at[:, :, 0:ROWS, 0:COLS], s_i.at[2]),
        pltpu.make_async_copy(guess_hbm, guess, s_i.at[3]),
    ]
    for copy in fetch:
        copy.start()
    column_groups = [lax.rem(tm + 4 * step, GROUPS) for step in range(1, 8)]
    for group in column_groups:
        greet(group, sx, sy)
    for step in range(4):
        group = 4 * z + lax.rem(x + step, 4)
        for core in (sx, 1 - sx):
            for column in (sy, west, east):
                if step > 0 or core is not sx or column is not sy:
                    greet(group, core, column)

    for copy in fetch:
        copy.wait()
    here = c_ref[tm]

    velx[:, :, 0:ROWS, 0:COLS] = vel[...].astype(F32)
    fld[0, :, 0:ROWS, 0:COLS] = guess[here]
    own = pl.ds(0, COLS)
    copies = [
        remote(srcx.at[:, :, edge, own], srcx.at[:, :, halo, own], s_a.at[0], r_a.at[0], (tm, 1 - sx, sy)),
        remote(velx.at[:, :, edge, own], velx.at[:, :, halo, own], s_a.at[1], r_a.at[1], (tm, 1 - sx, sy)),
        remote(fld.at[0, :, edge, own], fld.at[0, :, halo, own], s_a.at[2], r_a.at[2], (tm, 1 - sx, sy)),
    ]
    sides = ((True, slice(0, 128), west), (False, slice(COLS - 128, COLS), east))
    for way, (first_columns, lanes, target) in enumerate(sides):
        pairs = [(j, k) for j in range(STEPS) for k in range(2)]
        pk[way, 0] = pack_edges([lambda j=j, k=k: srcx[j, k, 0:ROWS, lanes] for j, k in pairs], first_columns)
        pk[way, 1] = pack_edges([lambda j=j, k=k: velx[j, k, 0:ROWS, lanes] for j, k in pairs], first_columns)
        pk[way, 2] = pack_edges([lambda k=k: fld[0, k, 0:ROWS, lanes] for k in range(2)], first_columns)
        copies.append(
            remote(pk.at[way], pkr.at[way, :, 0:ROWS], s_a.at[3 + way], r_a.at[3 + way], (tm, sx, target))
        )
        copies.append(
            remote(
                pk.at[way, :, edge], pkr.at[way, :, halo], s_a.at[5 + way], r_a.at[5 + way], (tm, 1 - sx, target)
            )
        )
    pl.semaphore_wait(barrier, 4 * 2 * 3 - 1 + 7)
    for copy in reversed(copies):
        copy.start()

    for group in column_groups:
        pl.semaphore_signal(known, inc=1, device_id=(group, sx, sy), device_id_type=MESH)

    def read_velocity(component, lane_tile):
        return vel[here, component, :, 128 * lane_tile : 128 * lane_tile + 128].astype(F32)

    half = pl.ds(pl.multiple_of(sx * ROWS, ROWS), ROWS)

    def is_self(index):
        return (owner_of(index) == tm) & (sx == 0)

    eighth = pl.ds(pl.multiple_of(sx * EDGE, EDGE), EDGE)

    def pack_ends(read, folded):
        folded[0] = fold(window(read, -1), -REACH)
        folded[1] = fold(window(read, TILES), REACH)

    def pack_window(read, source, index):
        source[index] = window(read, index).astype(source.dtype)

    def ends(folded, extras, send, recv):
        for side, target, device in ((0, west, owner_of(TILES - 1)), (1, east, owner_of(0))):
            yield remote(folded.at[side], extras.at[tm, eighth], send.at[TILES + side], recv(tm), (device, 0, target))

    def to_windows(source, boxes, send, recv, act):
        def one(turn, _):
            index = lax.rem(tile + turn, TILES)
            mine = is_self(index)

            @pl.when(mine)
            def _():
                if act:
                    pltpu.make_async_copy(source.at[index], boxes.at[tm, half], recv(tm)).start()

            @pl.when(jnp.logical_not(mine))
            def _():
                copy = remote(source.at[index], boxes.at[tm, half], send.at[index], recv(tm), (owner_of(index), 0, sy))
                copy.start() if act else copy.wait_send()

            return 0

        lax.fori_loop(0, TILES, one, 0)

    pack_ends(read_velocity, vf)
    for index in range(TILES):
        pack_window(read_velocity, vw, index)
    out[STEPS - 1] = guess[STEPS - 1]

    pl.semaphore_wait(known, 7)
    for copy in ends(vf, vxbuf, s_v, lambda g: r_v.at[g, 1]):
        copy.start()
    to_windows(vw, vbuf, s_v, lambda g: r_v.at[g, 0], True)
    for copy in copies:
        copy.wait()
    to_right = jnp.where(sy < 3, 1.0, 0.0).astype(F32)
    to_left = jnp.where(sy > 0, 1.0, 0.0).astype(F32)
    right = [pkr[0, part] * to_right for part in range(3)]
    left = [pkr[1, part] * to_left for part in range(3)]
    for j in range(STEPS):
        for k in range(2):
            srcx[j, k, :, COLS:XCOLS] = unpack_edges(right[0], left[0], 2 * j + k)
            velx[j, k, :, COLS:XCOLS] = unpack_edges(right[1], left[1], 2 * j + k)
    for k in range(2):
        fld[0, k, :, COLS:XCOLS] = unpack_edges(right[2], left[2], k)

    lane = iota((EDGE, XCOLS), 1)
    row = iota((EDGE, XCOLS), 0)
    inside = (lane < COLS) | ((lane < COLS + 64) & (sy < 3)) | ((lane >= COLS + 64) & (sy > 0))
    third = jnp.where(inside, 1.0 / 3.0, 0.0).astype(F32)
    tiles = XROWS // EDGE
    last_own = ROWS // EDGE - 1
    north_ok = jnp.where((row == EDGE - 1) & (sx == 1), 0.0, 1.0).astype(F32)
    south_ok = jnp.where((row == 0) & (sx == 0), 0.0, 1.0).astype(F32)

    def around(parts):
        up = [roll(part, -1, 0) for part in parts]
        down = [roll(part, 1, 0) for part in parts]
        for i, part in enumerate(parts):
            north = jnp.where(row == EDGE - 1, up[(i + 1) % tiles], up[i])
            south = jnp.where(row == 0, down[i - 1], down[i])
            yield part, north, south, roll(part, -1, 1), roll(part, 1, 1)

    def coefficients(j, _):
        u = [velx[j, 0, EDGE * i : EDGE * (i + 1), :] for i in range(tiles)]
        w = [velx[j, 1, EDGE * i : EDGE * (i + 1), :] for i in range(tiles)]
        for i, ((uc, un, us, ue, uw), (wc, wn, ws, we, ww)) in enumerate(zip(around(u), around(w))):
            rows = slice(EDGE * i, EDGE * (i + 1))
            scale_n = scale_s = third
            if i == last_own:
                un, wn, scale_n = un * north_ok, wn * north_ok, third * north_ok
            if i == 0:
                us, ws, scale_s = us * south_ok, ws * south_ok, third * south_ok
            hu, hw = 0.5 * uc, 0.5 * wc
            ht = 0.5 * third
            co1[j, 0, rows] = third - ht * (un - us)
            co1[j, 1, rows] = -ht * (wn - ws)
            co1[j, 2, rows] = third - ht * (we - ww)
            co1[j, 3, rows] = -ht * (ue - uw)
            co1[j, 4, rows] = scale_n * (0.5 + hu)
            co1[j, 5, rows] = scale_s * (0.5 - hu)
            co1[j, 6, rows] = third * (0.5 + hw)
            co1[j, 7, rows] = third * (0.5 - hw)
        return 0

    lax.fori_loop(0, STEPS - 1, coefficients, 0)

    def phi(field, slot, j):
        p = [field[slot, 0, EDGE * i : EDGE * (i + 1), :] for i in range(tiles)]
        q = [field[slot, 1, EDGE * i : EDGE * (i + 1), :] for i in range(tiles)]
        for i, ((pc, pn, ps, pe, pw), (qc, qn, qs, qe, qw)) in enumerate(zip(around(p), around(q))):
            rows = slice(EDGE * i, EDGE * (i + 1))
            a = [co1[j, n, rows] for n in range(8)]
            new_p = a[0] * pc + a[1] * qc + a[4] * pn + a[5] * ps + a[6] * pe + a[7] * pw + srcx[j, 0, rows]
            new_q = a[2] * qc + a[3] * pc + a[4] * qn + a[5] * qs + a[6] * qe + a[7] * qw + srcx[j, 1, rows]
            yield rows, i, ((0, pc, new_p), (1, qc, new_q))

    def lower(turn, _):
        j = STEPS - 2 - turn
        slot = lax.rem(turn, 2)
        active = j < here
        for rows, i, parts in phi(fld, slot, j):
            for k, old, new in parts:
                fld[1 - slot, k, rows] = jnp.where(active, new, old)
                if i <= last_own:
                    out[j, k, rows] = new[:, 0:COLS]
        return 0

    lax.fori_loop(0, STEPS - 1, lower, 0)
    done = (STEPS - 1) % 2

    relays = [
        remote(fld.at[done, :, 0:ROWS, own], nxt.at[0, :, 0:ROWS, own], s_b.at[0], r_b.at[0], (before, sx, sy)),
        remote(fld.at[done, :, edge, own], nxt.at[0, :, halo, own], s_b.at[1], r_b.at[1], (before, 1 - sx, sy)),
    ]
    for copy in relays:
        copy.start()
    for way, (first, lanes, target) in enumerate(
        ((True, slice(0, 128), west), (False, slice(COLS - 128, COLS), east))
    ):
        fp[way] = pack_edges([lambda k=k: fld[done, k, 0:ROWS, lanes] for k in range(2)], first)
        for copy in (
            remote(fp.at[way], fpr.at[way, 0:ROWS], s_b.at[2 + way], r_b.at[2 + way], (before, sx, target)),
            remote(fp.at[way, edge], fpr.at[way, halo], s_b.at[4 + way], r_b.at[4 + way], (before, 1 - sx, target)),
        ):
            copy.start()
            relays.append(copy)
    coefficients(STEPS - 1, 0)

    for copy in relays:
        copy.wait_recv()
    for k in range(2):
        nxt[0, k, :, COLS:XCOLS] = unpack_edges(fpr[0] * to_right, fpr[1] * to_left, k)

    @pl.when(tm == GROUPS - 1)
    def _():
        nxt[0] = jnp.zeros((2, XROWS, XCOLS), F32)

    def upper(turn, _):
        j = STEPS - 1 - turn
        slot = lax.rem(turn, 2)
        above = j > here
        coarse = j == here
        for rows, i, parts in phi(nxt, slot, j):
            for k, old, new in parts:
                nxt[1 - slot, k, rows] = jnp.where(above, new, old)
                if i <= last_own:
                    inner = new[:, 0:COLS]
                    out[j, k, rows] = jnp.where(above, inner, out[j, k, rows])
                    upd[k, rows] = jnp.where(coarse, inner, upd[k, rows])
        return 0

    upd[...] = jnp.zeros((2, ROWS, COLS), F32)
    lax.fori_loop(0, STEPS, upper, 0)

    res[...] = upd[...] - guess[here]

    def read_residual(component, lane_tile):
        return res[component, :, 128 * lane_tile : 128 * lane_tile + 128]

    pack_ends(read_residual, rf)
    for copy in ends(rf, xbuf, s_r, lambda g: r_rx.at[g]):
        copy.start()
    for index in range(TILES):
        pack_window(read_residual, rw, index)
    to_windows(rw, rbuf, s_r, lambda g: r_r.at[g], True)

    window_lane = iota((2 * ROWS, 128), 1)
    grid_row = iota((2 * ROWS, 128), 0)
    place = lax.rem(window_lane, 64)
    first = window_lane < 64
    from_extra = ((place < REACH) & (tile == 0)) | ((place >= 64 - REACH) & (tile == TILES - 1))
    outside = ((place < REACH) & (tile == 0) & (sy == 0)) | (
        (place >= 64 - REACH) & (tile == TILES - 1) & (sy == 3)
    )
    valid = (place[0 : ROWS // 2] >= REACH) & (place[0 : ROWS // 2] < 64 - REACH)
    keep = jnp.where(outside, 0.0, 1.0).astype(F32)
    top_open = jnp.where(grid_row == 2 * ROWS - 1, 0.0, 1.0).astype(F32)
    bottom_open = jnp.where(grid_row == 0, 0.0, 1.0).astype(F32)

    def unfold(part):
        pieces = [part[EDGE * core : EDGE * (core + 1)] for core in range(2)]
        step = jnp.where(tile == 0, 128 - REACH, REACH)
        return jnp.concatenate(
            [pltpu.roll(piece, lax.rem(step * i, 128), 1) for piece in pieces for i in range(ROWS // EDGE)], 0
        )

    @pl.when(is_owner)
    def _():
        def wait_velocity(level, _):
            arrived(vbuf.at[level], r_v.at[level, 0])
            return 0

        def merge(level, _):
            arrived(vxbuf.at[level], r_v.at[level, 1])
            both = jnp.where(from_extra, unfold(vxbuf[level]), vbuf[level].astype(F32))
            vbuf[level] = both.astype(jnp.bfloat16)
            return 0

        def coarse_coefficients(level, _):
            v = vbuf[level].astype(F32) * keep
            after = jnp.where(level + 1 < GROUPS, c_ref[jnp.minimum(level + 1, GROUPS - 1)], 0)
            span = jnp.full((1, 128), STEPS + after - c_ref[level], jnp.int32).astype(F32)
            inverse = keep * (1.0 / (1.0 + 2.0 * span))
            k = span * inverse
            swapped = roll(v, 64, 1)
            u = jnp.where(first, v, swapped)
            w = jnp.where(first, swapped, v)
            dx = 0.5 * (roll(v, -1, 0) * top_open - roll(v, 1, 0) * bottom_open)
            dy = 0.5 * (roll(v, -1, 1) - roll(v, 1, 1))
            coef[level, 0] = inverse - k * jnp.where(first, dx, dy)
            coef[level, 1] = -k * jnp.where(first, roll(dx, 64, 1), roll(dy, 64, 1))
            coef[level, 2] = k * (0.5 + 0.5 * u) * top_open
            coef[level, 3] = k * (0.5 - 0.5 * u) * bottom_open
            coef[level, 4] = k * (0.5 + 0.5 * w)
            coef[level, 5] = k * (0.5 - 0.5 * w)
            return 0

        def prepare(low, high):
            lax.fori_loop(low, high, wait_velocity, 0)

            @pl.when(is_end)
            def _():
                lax.fori_loop(low, high, merge, 0)

            lax.fori_loop(low, high, coarse_coefficients, 0)

        prepare(GROUPS - LEVELS, GROUPS)

        def send_error(level, core):
            own = (level == tm) & (core == 0)
            slot = jnp.where(own, TILES, tile)
            to_core = jnp.where(own, 1, core)
            return remote(
                ebuf.at[level, core], ebox.at[slot], s_e.at[level, core], r_e.at[slot], (level, to_core, sy)
            )

        def solve(top):
            def several(turn, error):
                first_level = top - BATCH * turn
                for n in range(BATCH):
                    arrived(rbuf.at[first_level - n], r_r.at[first_level - n])

                @pl.when(is_end)
                def _():
                    for n in range(BATCH):
                        level = first_level - n
                        arrived(xbuf.at[level], r_rx.at[level])
                        rbuf[level] = jnp.where(from_extra, unfold(xbuf[level]), rbuf[level])

                for n in range(BATCH):
                    level = first_level - n
                    c = [coef[level, n] for n in range(6)]
                    new = c[0] * error + c[1] * roll(error, 64, 1)
                    new = new + (c[2] * roll(error, -1, 0) + c[3] * roll(error, 1, 0))
                    new = new + (c[4] * roll(error, -1, 1) + c[5] * roll(error, 1, 1))
                    error = new + rbuf[level] * keep
                    for core in range(2):
                        low = new[ROWS * core : ROWS * core + ROWS // 2]
                        high = new[ROWS * core + ROWS // 2 : ROWS * (core + 1)]
                        piece = jnp.where(valid, low, roll(high, 32, 1))
                        ebuf[level, core] = piece
                        if core == 0:
                            ebox[tile] = jnp.where(level == tm, piece, ebox[tile])
                        send_error(level, core).start()
                return error

            return several

        error = lax.fori_loop(0, LEVELS // BATCH, solve(GROUPS - 1), jnp.zeros((2 * ROWS, 128), F32))
        mine[...] = error
        right_tile = lax.rem(tile + 1, TILES)
        left_tile = lax.rem(tile + TILES - 1, TILES)
        right_sy = jnp.where(tile == TILES - 1, east, sy)
        left_sy = jnp.where(tile == 0, west, sy)
        sides = [
            remote(mine, nbr.at[0], s_n.at[0], r_n.at[0], (owner_of(right_tile), 0, right_sy)),
            remote(mine, nbr.at[1], s_n.at[1], r_n.at[1], (owner_of(left_tile), 0, left_sy)),
        ]
        for copy in sides:
            copy.start()
        prepare(0, GROUPS - LEVELS)
        for copy in sides:
            copy.wait_recv()
        error = jnp.where(place < REACH, roll(nbr[0], -32, 1), error)
        error = jnp.where(place >= 64 - REACH, roll(nbr[1], 32, 1), error) * keep
        lax.fori_loop(0, LEVELS // BATCH, solve(GROUPS - LEVELS - 1), error)
        for copy in sides:
            copy.wait_send()

        def wait_errors(level, _):
            for core in range(2):
                send_error(level, core).wait_send()
            return 0

        lax.fori_loop(0, GROUPS, wait_errors, 0)

    def wait_boxes(index, _):
        pl.when(jnp.logical_not(is_owner & (index == tile)))(lambda: arrived(ebox.at[index], r_e.at[index]))
        return 0

    lax.fori_loop(0, TILES, wait_boxes, 0)

    @pl.when((sx == 1) & (lax.rem(x, 2) == lax.rem(z, 2)))
    def _():
        arrived(ebox.at[TILES], r_e.at[TILES])

    lane = iota((ROWS // 2, 128), 1)
    for part in range(2):
        rows = slice(part * ROWS // 2, (part + 1) * ROWS // 2)
        for k in range(2):
            for lane_tile in range(4):
                whole = None
                for i in range(4):
                    piece = roll(ebox[4 * lane_tile + i], 32 * i - REACH - 64 * k - 32 * part, 1)
                    whole = piece if whole is None else jnp.where(lane >= 32 * i, piece, whole)
                lanes = slice(128 * lane_tile, 128 * lane_tile + 128)
                upd[k, rows, lanes] = upd[k, rows, lanes] + whole

    def place_coarse(j, _):
        out[j] = jnp.where(j == here, upd[...], out[j])
        return 0

    lax.fori_loop(0, STEPS, place_coarse, 0)

    for copy in relays:
        copy.wait_send()
    for copy in (*ends(vf, vxbuf, s_v, lambda g: r_v.at[g, 1]), *ends(rf, xbuf, s_r, lambda g: r_rx.at[g])):
        copy.wait_send()
    to_windows(vw, vbuf, s_v, lambda g: r_v.at[g, 0], False)
    to_windows(rw, rbuf, s_r, lambda g: r_r.at[g], False)


def shards(adjoint_guess, sources, velocities, c_points):
    dma = pltpu.SemaphoreType.DMA
    vmem = pl.BlockSpec(memory_space=pltpu.VMEM)
    return pl.pallas_call(
        kernel,
        out_shape=jax.ShapeDtypeStruct(adjoint_guess.shape, F32),
        in_specs=[pl.BlockSpec(memory_space=pltpu.HBM)] * 4,
        out_specs=vmem,
        scratch_shapes=[
            pltpu.SMEM((GROUPS,), jnp.int32),
            pltpu.VMEM((STEPS, 2, ROWS, COLS), F32),
            pltpu.VMEM((STEPS, 2, ROWS, COLS), jnp.bfloat16),
            pltpu.VMEM((STEPS, 2, XROWS, XCOLS), F32),
            pltpu.VMEM((STEPS, 2, XROWS, XCOLS), F32),
            pltpu.VMEM((2, 2, XROWS, XCOLS), F32),
            pltpu.VMEM((2, 2, XROWS, XCOLS), F32),
            pltpu.VMEM((STEPS, 8, XROWS, XCOLS), F32),
            pltpu.VMEM((2, 3, ROWS, 128), F32),
            pltpu.VMEM((2, 3, XROWS, 128), F32),
            pltpu.VMEM((2, ROWS, 128), F32),
            pltpu.VMEM((2, XROWS, 128), F32),
            pltpu.VMEM((2, ROWS, COLS), F32),
            pltpu.VMEM((2, ROWS, COLS), F32),
            pltpu.VMEM((TILES, ROWS, 128), F32),
            pltpu.VMEM((2, EDGE, 128), F32),
            pltpu.VMEM((TILES, ROWS, 128), jnp.bfloat16),
            pltpu.VMEM((2, EDGE, 128), F32),
            pltpu.VMEM((GROUPS, 2 * ROWS, 128), F32),
            pltpu.VMEM((GROUPS, 2 * EDGE, 128), F32),
            pltpu.VMEM((GROUPS, 2 * ROWS, 128), jnp.bfloat16),
            pltpu.VMEM((GROUPS, 2 * EDGE, 128), F32),
            pltpu.VMEM((GROUPS, 6, 2 * ROWS, 128), F32),
            pltpu.VMEM((GROUPS, 2, ROWS // 2, 128), F32),
            pltpu.VMEM((TILES + 1, ROWS // 2, 128), F32),
            pltpu.VMEM((2 * ROWS, 128), F32),
            pltpu.VMEM((2, 2 * ROWS, 128), F32),
            dma((7,)), dma((7,)), dma((6,)), dma((6,)),
            dma((TILES + 2,)), dma((GROUPS, 2)),
            dma((TILES + 2,)), dma((GROUPS,)), dma((GROUPS,)),
            dma((GROUPS, 2)), dma((TILES + 1,)), dma((2,)), dma((2,)), dma((4,)), pltpu.SemaphoreType.REGULAR,
        ],
        compiler_params=pltpu.CompilerParams(has_side_effects=True, collective_id=0, vmem_limit_bytes=60 * 1024 * 1024),
    )(c_points, adjoint_guess, sources, velocities)


def solution(mesh):
    placed = (P("tm", None, "sx", "sy"), P("tm", None, "sx", "sy"), P("tm", None, "sx", "sy"), P())
    return jax.shard_map(
        shards, mesh=mesh, in_specs=placed, out_specs=P("tm", None, "sx", "sy"), check_vma=False
    )
```

time: 78.3 us -> 58.5 us (0.75)
  Pallas kernels: 72.9 us -> 56.1 us
  local copies, waits for them, and re-layouts: 5.12 us -> 2.29 us
    pallas_call x1, Pallas kernels: 72.9 us -> 56.1 us  [shards(): pl.pallas_call(kernel, out_shape=jax.ShapeDtypeStruct(adjoint_guess.shape...]
    unnamed x9 -> x1, local copies, waits for them, and re-layouts: 5.12 us -> 2.29 us
where the time goes in v2:
time: 58.5 us; the launch traced here: 58.4 us
  Pallas kernels  56.1 us (96%)
  local copies, waits for them, and re-layouts  2.29 us (4%)
    pallas_call x1, Pallas kernels, shards(): pl.pallas_call(kernel, out_shape=jax.ShapeDtypeStruct(adjoint_guess.shape...  56.1 us
    unnamed x1, local copies, waits for them, and re-layouts  2.29 us

profile of v2, /device:TPU:1, one launch (start us, length us, event | category | flops | bytes accessed | tf_op | source)
XLA Modules:
  0.0 58.4 jit_solution(13465116413455614531)
XLA Ops:
  0.0 56.1 %shard_map.46 = f32[8,2,32,512]{3,2,1,0:T(8,128)} custom-call(s32[32]{0:T(128)} %c_hbm.1, f32[8,2,32,512]{3,2,1,0:T(8,128)} %guess_hbm.1, f32[8,2,32,512]{3,2,1,0:T(8,128)} %src_hbm.1, bf16[8,2,32,512]{3,2,1,0:T(8,128)(2,1)} %vel_hbm.1), custom_call_target="tpu_custom_call" | custom-call | tf_op jit(solution)/shard_map/pallas_call | solution.py:513
  56.1 2.3 %copy.6 = f32[8,2,32,512]{3,2,1,0:T(8,128)} copy(f32[8,2,32,512]{3,2,1,0:T(8,128)} %shard_map.46) | data formatting | bytes 2097152

commit v3 on v2

--- a/solution.py
+++ b/solution.py
@@ -15,6 +15,7 @@
 XCOLS = COLS + 128
 GROUPS = 32
 TILES = 16
+WHOLE = 32000.0
 REACH = 16
 BATCH = 4
 LEVELS = 16
@@ -74,9 +75,9 @@
 
 def kernel(
     c_hbm, guess_hbm, src_hbm, vel_hbm, out,
-    c_ref, guess, vel, srcx, velx, fld, nxt, co1, pk, pkr, fp, fpr, res, upd, rw, rf, vw, vf,
-    rbuf, xbuf, vbuf, vxbuf, coef, ebuf, ebox, mine, nbr,
-    s_a, r_a, s_b, r_b, s_v, r_v, s_r, r_r, r_rx, s_e, r_e, s_n, r_n, s_i, known,
+    c_ref, guess, vel, srcx, velx, fld, nxt, co1, pk, pkr, fp, fpr, fq, nq, fs, ns, ff, nf, res, upd, rw, rf, vw, vf,
+    rbuf, xbuf, vbuf, vxbuf, coef, dec, ebuf, ebox, mine, nbr,
+    s_a, r_a, s_b, r_b, s_v, r_v, r_vx, s_r, r_r, r_rx, s_e, r_e, s_n, r_n, s_i, known,
 ):
     tm = lax.axis_index("tm")
     sx = lax.axis_index("sx")
@@ -172,9 +173,6 @@
         folded[0] = fold(window(read, -1), -REACH)
         folded[1] = fold(window(read, TILES), REACH)
 
-    def pack_window(read, source, index):
-        source[index] = window(read, index).astype(source.dtype)
-
     def ends(folded, extras, send, recv):
         for side, target, device in ((0, west, owner_of(TILES - 1)), (1, east, owner_of(0))):
             yield remote(folded.at[side], extras.at[tm, eighth], send.at[TILES + side], recv(tm), (device, 0, target))
@@ -200,13 +198,13 @@
 
     pack_ends(read_velocity, vf)
     for index in range(TILES):
-        pack_window(read_velocity, vw, index)
+        vw[index] = window(read_velocity, index).astype(jnp.bfloat16)
     out[STEPS - 1] = guess[STEPS - 1]
 
     pl.semaphore_wait(known, 7)
-    for copy in ends(vf, vxbuf, s_v, lambda g: r_v.at[g, 1]):
+    for copy in ends(vf, vxbuf, s_v, lambda g: r_vx.at[g]):
         copy.start()
-    to_windows(vw, vbuf, s_v, lambda g: r_v.at[g, 0], True)
+    to_windows(vw, vbuf, s_v, lambda g: r_v.at[g // LEVELS], True)
     for copy in copies:
         copy.wait()
     to_right = jnp.where(sy < 3, 1.0, 0.0).astype(F32)
@@ -285,28 +283,55 @@
     lax.fori_loop(0, STEPS - 1, lower, 0)
     done = (STEPS - 1) % 2
 
+    largest = jnp.max(jnp.abs(fld[done, :, 0:ROWS, 0:COLS]), axis=(0, 2))[:, None]
+    power = jnp.floor(8.0 * jnp.log2(jnp.maximum(largest, 1e-30))) + 2.0
+    to_unit = WHOLE * jnp.exp2(-0.125 * power)
+    for k in range(2):
+        fq[k] = jnp.floor(fld[done, k, 0:ROWS, 0:COLS] * to_unit + 0.5).astype(jnp.int32).astype(jnp.int16)
+    quarter = iota((EDGE, 128), 1) // 32
+    spread = jnp.broadcast_to(power, (ROWS, 128))
+    scales = spread[0:EDGE]
+    for i in range(1, ROWS // EDGE):
+        scales = jnp.where(quarter == i, spread[EDGE * i : EDGE * (i + 1)], scales)
+    fs[...] = scales
     relays = [
-        remote(fld.at[done, :, 0:ROWS, own], nxt.at[0, :, 0:ROWS, own], s_b.at[0], r_b.at[0], (before, sx, sy)),
         remote(fld.at[done, :, edge, own], nxt.at[0, :, halo, own], s_b.at[1], r_b.at[1], (before, 1 - sx, sy)),
+        remote(fq, nq, s_b.at[0], r_b.at[0], (before, sx, sy)),
+        remote(fs, ns, s_b.at[6], r_b.at[6], (before, sx, sy)),
     ]
-    for copy in relays:
+    for way, (first_columns, lanes, target) in enumerate(sides):
+        fp[way] = pack_edges([lambda k=k: fld[done, k, 0:ROWS, lanes] for k in range(2)], first_columns)
+        sixteenth = iota((EDGE, 128), 1) // (2 * EDGE)
+        folded = fp[way, 0:EDGE]
+        for i in range(1, ROWS // EDGE):
+            moved = roll(fp[way, EDGE * i : EDGE * (i + 1)], 2 * EDGE * i, 1)
+            folded = jnp.where(sixteenth == i, moved, folded)
+        ff[way] = folded
+        relays.append(remote(ff.at[way], nf.at[way], s_b.at[2 + way], r_b.at[2 + way], (before, sx, target)))
+        relays.append(
+            remote(fp.at[way, edge], fpr.at[way], s_b.at[4 + way], r_b.at[4 + way], (before, 1 - sx, target))
+        )
+    for copy in reversed(relays):
         copy.start()
-    for way, (first, lanes, target) in enumerate(
-        ((True, slice(0, 128), west), (False, slice(COLS - 128, COLS), east))
-    ):
-        fp[way] = pack_edges([lambda k=k: fld[done, k, 0:ROWS, lanes] for k in range(2)], first)
-        for copy in (
-            remote(fp.at[way], fpr.at[way, 0:ROWS], s_b.at[2 + way], r_b.at[2 + way], (before, sx, target)),
-            remote(fp.at[way, edge], fpr.at[way, halo], s_b.at[4 + way], r_b.at[4 + way], (before, 1 - sx, target)),
-        ):
-            copy.start()
-            relays.append(copy)
     coefficients(STEPS - 1, 0)
 
     for copy in relays:
         copy.wait_recv()
+    got = [
+        jnp.concatenate([roll(nf[way], -2 * EDGE * i, 1) for i in range(ROWS // EDGE)] + [fpr[way]], 0)
+        for way in range(2)
+    ]
     for k in range(2):
-        nxt[0, k, :, COLS:XCOLS] = unpack_edges(fpr[0] * to_right, fpr[1] * to_left, k)
+        nxt[0, k, :, COLS:XCOLS] = unpack_edges(got[0] * to_right, got[1] * to_left, k)
+    scales = ns[...]
+    unit = jnp.concatenate(
+        [jnp.broadcast_to(scales[:, 32 * i : 32 * i + 1], (EDGE, 128)) for i in range(ROWS // EDGE)], 0
+    )
+    unit = jnp.exp2(0.125 * unit) * (1.0 / WHOLE)
+    for k in range(2):
+        for lane_tile in range(COLS // 128):
+            lanes = slice(128 * lane_tile, 128 * lane_tile + 128)
+            nxt[0, k, 0:ROWS, lanes] = nq[k, :, lanes].astype(jnp.int32).astype(F32) * unit
 
     @pl.when(tm == GROUPS - 1)
     def _():
@@ -337,9 +362,15 @@
     pack_ends(read_residual, rf)
     for copy in ends(rf, xbuf, s_r, lambda g: r_rx.at[g]):
         copy.start()
+    largest = jnp.max(jnp.abs(res[...]), axis=(0, 2))[:, None]
+    power = jnp.floor(8.0 * jnp.log2(jnp.maximum(largest, 1e-30))) + 2.0
+    power = jnp.broadcast_to(power, (ROWS, 128))
+    to_unit = WHOLE * jnp.exp2(-0.125 * power)
+    first_lane = iota((ROWS, 128), 1) == 0
     for index in range(TILES):
-        pack_window(read_residual, rw, index)
-    to_windows(rw, rbuf, s_r, lambda g: r_r.at[g], True)
+        piece = jnp.floor(window(read_residual, index) * to_unit + 0.5)
+        rw[index] = jnp.where(first_lane, power, piece).astype(jnp.int32).astype(jnp.int16)
+    to_windows(rw, rbuf, s_r, lambda g: r_r.at[g // BATCH], True)
 
     window_lane = iota((2 * ROWS, 128), 1)
     grid_row = iota((2 * ROWS, 128), 0)
@@ -363,12 +394,8 @@
 
     @pl.when(is_owner)
     def _():
-        def wait_velocity(level, _):
-            arrived(vbuf.at[level], r_v.at[level, 0])
-            return 0
-
         def merge(level, _):
-            arrived(vxbuf.at[level], r_v.at[level, 1])
+            arrived(vxbuf.at[level], r_vx.at[level])
             both = jnp.where(from_extra, unfold(vxbuf[level]), vbuf[level].astype(F32))
             vbuf[level] = both.astype(jnp.bfloat16)
             return 0
@@ -393,7 +420,7 @@
             return 0
 
         def prepare(low, high):
-            lax.fori_loop(low, high, wait_velocity, 0)
+            arrived(vbuf.at[low:high], r_v.at[low // LEVELS])
 
             @pl.when(is_end)
             def _():
@@ -414,23 +441,27 @@
         def solve(top):
             def several(turn, error):
                 first_level = top - BATCH * turn
+                last_level = first_level - BATCH + 1
+                arrived(rbuf.at[pl.ds(last_level, BATCH)], r_r.at[last_level // BATCH])
                 for n in range(BATCH):
-                    arrived(rbuf.at[first_level - n], r_r.at[first_level - n])
+                    whole = rbuf[first_level - n].astype(jnp.int32).astype(F32)
+                    unit = jnp.exp2(0.125 * jnp.broadcast_to(whole[:, 0:1], whole.shape)) * (1.0 / WHOLE)
+                    dec[n] = whole * unit * keep
 
                 @pl.when(is_end)
                 def _():
                     for n in range(BATCH):
                         level = first_level - n
                         arrived(xbuf.at[level], r_rx.at[level])
-                        rbuf[level] = jnp.where(from_extra, unfold(xbuf[level]), rbuf[level])
+                        dec[n] = jnp.where(from_extra, unfold(xbuf[level]) * keep, dec[n])
 
                 for n in range(BATCH):
                     level = first_level - n
-                    c = [coef[level, n] for n in range(6)]
+                    c = [coef[level, i] for i in range(6)]
                     new = c[0] * error + c[1] * roll(error, 64, 1)
                     new = new + (c[2] * roll(error, -1, 0) + c[3] * roll(error, 1, 0))
                     new = new + (c[4] * roll(error, -1, 1) + c[5] * roll(error, 1, 1))
-                    error = new + rbuf[level] * keep
+                    error = new + dec[n]
                     for core in range(2):
                         low = new[ROWS * core : ROWS * core + ROWS // 2]
                         high = new[ROWS * core + ROWS // 2 : ROWS * (core + 1)]
@@ -501,10 +532,10 @@
 
     for copy in relays:
         copy.wait_send()
-    for copy in (*ends(vf, vxbuf, s_v, lambda g: r_v.at[g, 1]), *ends(rf, xbuf, s_r, lambda g: r_rx.at[g])):
+    for copy in (*ends(vf, vxbuf, s_v, lambda g: r_vx.at[g]), *ends(rf, xbuf, s_r, lambda g: r_rx.at[g])):
         copy.wait_send()
-    to_windows(vw, vbuf, s_v, lambda g: r_v.at[g, 0], False)
-    to_windows(rw, rbuf, s_r, lambda g: r_r.at[g], False)
+    to_windows(vw, vbuf, s_v, lambda g: r_v.at[g // LEVELS], False)
+    to_windows(rw, rbuf, s_r, lambda g: r_r.at[g // BATCH], False)
 
 
 def shards(adjoint_guess, sources, velocities, c_points):
@@ -512,7 +543,7 @@
     vmem = pl.BlockSpec(memory_space=pltpu.VMEM)
     return pl.pallas_call(
         kernel,
-        out_shape=jax.ShapeDtypeStruct(adjoint_guess.shape, F32),
+        out_shape=pltpu.VMEM(adjoint_guess.shape, F32),
         in_specs=[pl.BlockSpec(memory_space=pltpu.HBM)] * 4,
         out_specs=vmem,
         scratch_shapes=[
@@ -527,28 +558,35 @@
             pltpu.VMEM((2, 3, ROWS, 128), F32),
             pltpu.VMEM((2, 3, XROWS, 128), F32),
             pltpu.VMEM((2, ROWS, 128), F32),
-            pltpu.VMEM((2, XROWS, 128), F32),
+            pltpu.VMEM((2, EDGE, 128), F32),
+            pltpu.VMEM((2, ROWS, COLS), jnp.int16),
+            pltpu.VMEM((2, ROWS, COLS), jnp.int16),
+            pltpu.VMEM((EDGE, 128), F32),
+            pltpu.VMEM((EDGE, 128), F32),
+            pltpu.VMEM((2, EDGE, 128), F32),
+            pltpu.VMEM((2, EDGE, 128), F32),
             pltpu.VMEM((2, ROWS, COLS), F32),
             pltpu.VMEM((2, ROWS, COLS), F32),
-            pltpu.VMEM((TILES, ROWS, 128), F32),
+            pltpu.VMEM((TILES, ROWS, 128), jnp.int16),
             pltpu.VMEM((2, EDGE, 128), F32),
             pltpu.VMEM((TILES, ROWS, 128), jnp.bfloat16),
             pltpu.VMEM((2, EDGE, 128), F32),
-            pltpu.VMEM((GROUPS, 2 * ROWS, 128), F32),
+            pltpu.VMEM((GROUPS, 2 * ROWS, 128), jnp.int16),
             pltpu.VMEM((GROUPS, 2 * EDGE, 128), F32),
             pltpu.VMEM((GROUPS, 2 * ROWS, 128), jnp.bfloat16),
             pltpu.VMEM((GROUPS, 2 * EDGE, 128), F32),
             pltpu.VMEM((GROUPS, 6, 2 * ROWS, 128), F32),
+            pltpu.VMEM((BATCH, 2 * ROWS, 128), F32),
             pltpu.VMEM((GROUPS, 2, ROWS // 2, 128), F32),
             pltpu.VMEM((TILES + 1, ROWS // 2, 128), F32),
             pltpu.VMEM((2 * ROWS, 128), F32),
             pltpu.VMEM((2, 2 * ROWS, 128), F32),
-            dma((7,)), dma((7,)), dma((6,)), dma((6,)),
-            dma((TILES + 2,)), dma((GROUPS, 2)),
-            dma((TILES + 2,)), dma((GROUPS,)), dma((GROUPS,)),
+            dma((7,)), dma((7,)), dma((7,)), dma((7,)),
+            dma((TILES + 2,)), dma((GROUPS // LEVELS,)), dma((GROUPS,)),
+            dma((TILES + 2,)), dma((GROUPS // BATCH,)), dma((GROUPS,)),
             dma((GROUPS, 2)), dma((TILES + 1,)), dma((2,)), dma((2,)), dma((4,)), pltpu.SemaphoreType.REGULAR,
         ],
-        compiler_params=pltpu.CompilerParams(has_side_effects=True, collective_id=0, vmem_limit_bytes=60 * 1024 * 1024),
+        compiler_params=pltpu.CompilerParams(has_side_effects=True, collective_id=0, vmem_limit_bytes=58 * 1024 * 1024),
     )(c_points, adjoint_guess, sources, velocities)
 
 

time: 58.5 us -> 51.5 us (0.88)
  Pallas kernels: 56.1 us -> 50.4 us
  local copies, waits for them, and re-layouts: 2.29 us -> 0.97 us
    pallas_call x1, Pallas kernels: 56.1 us -> 50.4 us  [shards(): pl.pallas_call(kernel, out_shape=pltpu.VMEM(adjoint_guess.shape, F32), in...]
    unnamed x1, local copies, waits for them, and re-layouts: 2.29 us -> 0.97 us
where the time goes in v3:
time: 51.5 us; the launch traced here: 51.3 us
  Pallas kernels  50.4 us (98%)
  local copies, waits for them, and re-layouts  0.97 us (2%)
    pallas_call x1, Pallas kernels, shards(): pl.pallas_call(kernel, out_shape=pltpu.VMEM(adjoint_guess.shape, F32), in...  50.4 us

profile of v3, /device:TPU:1, one launch (start us, length us, event | category | flops | bytes accessed | tf_op | source)
XLA Modules:
  0.0 51.3 jit_solution(12131060299594498178)
XLA Ops:
  0.0 50.4 %shard_map.46 = f32[8,2,32,512]{3,2,1,0:T(8,128)S(1)} custom-call(s32[32]{0:T(128)} %c_hbm.1, f32[8,2,32,512]{3,2,1,0:T(8,128)} %guess_hbm.1, f32[8,2,32,512]{3,2,1,0:T(8,128)} %src_hbm.1, bf16[8,2,32,512]{3,2,1,0:T(8,128)(2,1)} %vel_hbm.1), custom_call_target="tpu_custom_call" | custom-call | tf_op jit(solution)/shard_map/pallas_call | solution.py:544
  50.4 1.0 %copy.6 = f32[8,2,32,512]{3,2,1,0:T(8,128)} copy(f32[8,2,32,512]{3,2,1,0:T(8,128)S(1)} %shard_map.46) | data formatting | bytes 2097152

commit v4 on v3

--- a/solution.py
+++ b/solution.py
@@ -29,20 +29,20 @@
     return pltpu.roll(x, shift % x.shape[dim], dim)
 
 
-def pack_edges(tiles, first):
+def pack_edges(firsts, lasts):
     lane = iota((ROWS, 128), 1)
-    packed = jnp.zeros((ROWS, 128), F32)
-    for place, tile in enumerate(tiles):
+    to_west = to_east = jnp.zeros((ROWS, 128), F32)
+    for place, (first, last) in enumerate(zip(firsts, lasts)):
         at = EDGE * place
-        moved = roll(tile(), at if first else at + EDGE, 1)
-        packed = jnp.where((lane >= at) & (lane < at + EDGE), moved, packed)
-    return packed
+        moved = roll(jnp.where(lane < 64, first(), last()), at, 1)
+        to_west = jnp.where(lane // EDGE == place, moved, to_west)
+        to_east = jnp.where(lane // EDGE == (place - 1) % 16, moved, to_east)
+    return to_west, to_east
 
 
 def unpack_edges(right, left, place):
-    lane = iota((XROWS, 128), 1)
-    at = EDGE * place
-    return jnp.where(lane < 64, roll(right, -at, 1), roll(left, -EDGE - at, 1))
+    group = iota((XROWS, 128), 1) // EDGE
+    return roll(jnp.where(group == place, right, left), -EDGE * place, 1)
 
 
 def window(read, index):
@@ -126,24 +126,31 @@
                 if step > 0 or core is not sx or column is not sy:
                     greet(group, core, column)
 
-    for copy in fetch:
+    for copy in fetch[:2]:
         copy.wait()
     here = c_ref[tm]
 
     velx[:, :, 0:ROWS, 0:COLS] = vel[...].astype(F32)
+    own = pl.ds(0, COLS)
+    head = slice(0, 128)
+    tail = slice(COLS - 128, COLS)
+    pairs = [(j, k) for j in range(STEPS) for k in range(2)]
+
+    def edges_of(array, count):
+        return [[lambda j=j, k=k, lanes=lanes: array[j, k, 0:ROWS, lanes] for j, k in count] for lanes in (head, tail)]
+
+    pk[0, 1], pk[1, 1] = pack_edges(*edges_of(velx, pairs))
+    fetch[3].wait()
     fld[0, :, 0:ROWS, 0:COLS] = guess[here]
-    own = pl.ds(0, COLS)
+    pk[0, 2], pk[1, 2] = pack_edges(*edges_of(fld, [(0, 0), (0, 1)]))
+    fetch[2].wait()
+    pk[0, 0], pk[1, 0] = pack_edges(*edges_of(srcx, pairs))
     copies = [
         remote(srcx.at[:, :, edge, own], srcx.at[:, :, halo, own], s_a.at[0], r_a.at[0], (tm, 1 - sx, sy)),
         remote(velx.at[:, :, edge, own], velx.at[:, :, halo, own], s_a.at[1], r_a.at[1], (tm, 1 - sx, sy)),
         remote(fld.at[0, :, edge, own], fld.at[0, :, halo, own], s_a.at[2], r_a.at[2], (tm, 1 - sx, sy)),
     ]
-    sides = ((True, slice(0, 128), west), (False, slice(COLS - 128, COLS), east))
-    for way, (first_columns, lanes, target) in enumerate(sides):
-        pairs = [(j, k) for j in range(STEPS) for k in range(2)]
-        pk[way, 0] = pack_edges([lambda j=j, k=k: srcx[j, k, 0:ROWS, lanes] for j, k in pairs], first_columns)
-        pk[way, 1] = pack_edges([lambda j=j, k=k: velx[j, k, 0:ROWS, lanes] for j, k in pairs], first_columns)
-        pk[way, 2] = pack_edges([lambda k=k: fld[0, k, 0:ROWS, lanes] for k in range(2)], first_columns)
+    for way, target in enumerate((west, east)):
         copies.append(
             remote(pk.at[way], pkr.at[way, :, 0:ROWS], s_a.at[3 + way], r_a.at[3 + way], (tm, sx, target))
         )
@@ -164,9 +171,6 @@
 
     half = pl.ds(pl.multiple_of(sx * ROWS, ROWS), ROWS)
 
-    def is_self(index):
-        return (owner_of(index) == tm) & (sx == 0)
-
     eighth = pl.ds(pl.multiple_of(sx * EDGE, EDGE), EDGE)
 
     def pack_ends(read, folded):
@@ -178,23 +182,24 @@
             yield remote(folded.at[side], extras.at[tm, eighth], send.at[TILES + side], recv(tm), (device, 0, target))
 
     def to_windows(source, boxes, send, recv, act):
-        def one(turn, _):
+        for turn in range(TILES):
             index = lax.rem(tile + turn, TILES)
-            mine = is_self(index)
-
-            @pl.when(mine)
+            mine = (owner_of(index) == tm) & (sx == 0)
+            slot = jnp.where(mine, GROUPS, tm)
+            to_core = jnp.where(mine, 1, 0)
+            copy = remote(
+                source.at[index], boxes.at[slot, half], send.at[index], recv(slot), (owner_of(index), to_core, sy)
+            )
+            copy.start() if act else copy.wait_send()
+        if act:
+
+            @pl.when(is_owner)
             def _():
-                if act:
-                    pltpu.make_async_copy(source.at[index], boxes.at[tm, half], recv(tm)).start()
-
-            @pl.when(jnp.logical_not(mine))
-            def _():
-                copy = remote(source.at[index], boxes.at[tm, half], send.at[index], recv(tm), (owner_of(index), 0, sy))
-                copy.start() if act else copy.wait_send()
-
-            return 0
-
-        lax.fori_loop(0, TILES, one, 0)
+                pltpu.make_async_copy(source.at[tile], boxes.at[tm, half], recv(tm)).start()
+
+    def unused_windows(boxes, recv):
+        rows = pl.ds(0, ROWS)
+        arrived(boxes.at[GROUPS, rows], recv(GROUPS))
 
     pack_ends(read_velocity, vf)
     for index in range(TILES):
@@ -299,12 +304,12 @@
         remote(fq, nq, s_b.at[0], r_b.at[0], (before, sx, sy)),
         remote(fs, ns, s_b.at[6], r_b.at[6], (before, sx, sy)),
     ]
-    for way, (first_columns, lanes, target) in enumerate(sides):
-        fp[way] = pack_edges([lambda k=k: fld[done, k, 0:ROWS, lanes] for k in range(2)], first_columns)
+    fp[0], fp[1] = pack_edges(*edges_of(fld, [(done, 0), (done, 1)]))
+    for way, target in enumerate((west, east)):
         sixteenth = iota((EDGE, 128), 1) // (2 * EDGE)
-        folded = fp[way, 0:EDGE]
+        folded = roll(fp[way, 0:EDGE], EDGE * way, 1)
         for i in range(1, ROWS // EDGE):
-            moved = roll(fp[way, EDGE * i : EDGE * (i + 1)], 2 * EDGE * i, 1)
+            moved = roll(fp[way, EDGE * i : EDGE * (i + 1)], EDGE * (2 * i + way), 1)
             folded = jnp.where(sixteenth == i, moved, folded)
         ff[way] = folded
         relays.append(remote(ff.at[way], nf.at[way], s_b.at[2 + way], r_b.at[2 + way], (before, sx, target)))
@@ -318,7 +323,7 @@
     for copy in relays:
         copy.wait_recv()
     got = [
-        jnp.concatenate([roll(nf[way], -2 * EDGE * i, 1) for i in range(ROWS // EDGE)] + [fpr[way]], 0)
+        jnp.concatenate([roll(nf[way], -EDGE * (2 * i + way), 1) for i in range(ROWS // EDGE)] + [fpr[way]], 0)
         for way in range(2)
     ]
     for k in range(2):
@@ -371,6 +376,23 @@
         piece = jnp.floor(window(read_residual, index) * to_unit + 0.5)
         rw[index] = jnp.where(first_lane, power, piece).astype(jnp.int32).astype(jnp.int16)
     to_windows(rw, rbuf, s_r, lambda g: r_r.at[g // BATCH], True)
+
+    def send_error(level, core):
+        own = (level == tm) & (core == 0)
+        slot = jnp.where(own, TILES, tile)
+        to_core = jnp.where(own, 1, core)
+        return remote(
+            ebuf.at[level, core], ebox.at[slot], s_e.at[level, core], r_e.at[slot], (level, to_core, sy)
+        )
+
+    right_tile = lax.rem(tile + 1, TILES)
+    left_tile = lax.rem(tile + TILES - 1, TILES)
+    right_sy = jnp.where(tile == TILES - 1, east, sy)
+    left_sy = jnp.where(tile == 0, west, sy)
+    refresh = [
+        remote(mine, nbr.at[0], s_n.at[0], r_n.at[0], (owner_of(right_tile), 0, right_sy)),
+        remote(mine, nbr.at[1], s_n.at[1], r_n.at[1], (owner_of(left_tile), 0, left_sy)),
+    ]
 
     window_lane = iota((2 * ROWS, 128), 1)
     grid_row = iota((2 * ROWS, 128), 0)
@@ -430,14 +452,6 @@
 
         prepare(GROUPS - LEVELS, GROUPS)
 
-        def send_error(level, core):
-            own = (level == tm) & (core == 0)
-            slot = jnp.where(own, TILES, tile)
-            to_core = jnp.where(own, 1, core)
-            return remote(
-                ebuf.at[level, core], ebox.at[slot], s_e.at[level, core], r_e.at[slot], (level, to_core, sy)
-            )
-
         def solve(top):
             def several(turn, error):
                 first_level = top - BATCH * turn
@@ -476,31 +490,27 @@
 
         error = lax.fori_loop(0, LEVELS // BATCH, solve(GROUPS - 1), jnp.zeros((2 * ROWS, 128), F32))
         mine[...] = error
-        right_tile = lax.rem(tile + 1, TILES)
-        left_tile = lax.rem(tile + TILES - 1, TILES)
-        right_sy = jnp.where(tile == TILES - 1, east, sy)
-        left_sy = jnp.where(tile == 0, west, sy)
-        sides = [
-            remote(mine, nbr.at[0], s_n.at[0], r_n.at[0], (owner_of(right_tile), 0, right_sy)),
-            remote(mine, nbr.at[1], s_n.at[1], r_n.at[1], (owner_of(left_tile), 0, left_sy)),
-        ]
-        for copy in sides:
+        for copy in refresh:
             copy.start()
         prepare(0, GROUPS - LEVELS)
-        for copy in sides:
+        for copy in refresh:
             copy.wait_recv()
         error = jnp.where(place < REACH, roll(nbr[0], -32, 1), error)
         error = jnp.where(place >= 64 - REACH, roll(nbr[1], 32, 1), error) * keep
         lax.fori_loop(0, LEVELS // BATCH, solve(GROUPS - LEVELS - 1), error)
-        for copy in sides:
-            copy.wait_send()
-
-        def wait_errors(level, _):
-            for core in range(2):
-                send_error(level, core).wait_send()
-            return 0
-
-        lax.fori_loop(0, GROUPS, wait_errors, 0)
+
+    for copy in relays:
+        copy.wait_send()
+    for copy in (*ends(vf, vxbuf, s_v, lambda g: r_vx.at[g]), *ends(rf, xbuf, s_r, lambda g: r_rx.at[g])):
+        copy.wait_send()
+    to_windows(vw, vbuf, s_v, lambda g: r_v.at[g // LEVELS], False)
+    to_windows(rw, rbuf, s_r, lambda g: r_r.at[g // BATCH], False)
+    owner_chip = lax.rem(x, 2) == lax.rem(z, 2)
+
+    @pl.when((sx == 1) & owner_chip)
+    def _():
+        unused_windows(vbuf, lambda g: r_v.at[g // LEVELS])
+        unused_windows(rbuf, lambda g: r_r.at[g // BATCH])
 
     def wait_boxes(index, _):
         pl.when(jnp.logical_not(is_owner & (index == tile)))(lambda: arrived(ebox.at[index], r_e.at[index]))
@@ -508,7 +518,7 @@
 
     lax.fori_loop(0, TILES, wait_boxes, 0)
 
-    @pl.when((sx == 1) & (lax.rem(x, 2) == lax.rem(z, 2)))
+    @pl.when((sx == 1) & owner_chip)
     def _():
         arrived(ebox.at[TILES], r_e.at[TILES])
 
@@ -530,12 +540,17 @@
 
     lax.fori_loop(0, STEPS, place_coarse, 0)
 
-    for copy in relays:
-        copy.wait_send()
-    for copy in (*ends(vf, vxbuf, s_v, lambda g: r_vx.at[g]), *ends(rf, xbuf, s_r, lambda g: r_rx.at[g])):
-        copy.wait_send()
-    to_windows(vw, vbuf, s_v, lambda g: r_v.at[g // LEVELS], False)
-    to_windows(rw, rbuf, s_r, lambda g: r_r.at[g // BATCH], False)
+    @pl.when(is_owner)
+    def _():
+        for copy in refresh:
+            copy.wait_send()
+
+        def wait_errors(level, _):
+            for core in range(2):
+                send_error(level, core).wait_send()
+            return 0
+
+        lax.fori_loop(0, GROUPS, wait_errors, 0)
 
 
 def shards(adjoint_guess, sources, velocities, c_points):
@@ -571,9 +586,9 @@
             pltpu.VMEM((2, EDGE, 128), F32),
             pltpu.VMEM((TILES, ROWS, 128), jnp.bfloat16),
             pltpu.VMEM((2, EDGE, 128), F32),
-            pltpu.VMEM((GROUPS, 2 * ROWS, 128), jnp.int16),
+            pltpu.VMEM((GROUPS + 1, 2 * ROWS, 128), jnp.int16),
             pltpu.VMEM((GROUPS, 2 * EDGE, 128), F32),
-            pltpu.VMEM((GROUPS, 2 * ROWS, 128), jnp.bfloat16),
+            pltpu.VMEM((GROUPS + 1, 2 * ROWS, 128), jnp.bfloat16),
             pltpu.VMEM((GROUPS, 2 * EDGE, 128), F32),
             pltpu.VMEM((GROUPS, 6, 2 * ROWS, 128), F32),
             pltpu.VMEM((BATCH, 2 * ROWS, 128), F32),
@@ -582,8 +597,8 @@
             pltpu.VMEM((2 * ROWS, 128), F32),
             pltpu.VMEM((2, 2 * ROWS, 128), F32),
             dma((7,)), dma((7,)), dma((7,)), dma((7,)),
-            dma((TILES + 2,)), dma((GROUPS // LEVELS,)), dma((GROUPS,)),
-            dma((TILES + 2,)), dma((GROUPS // BATCH,)), dma((GROUPS,)),
+            dma((TILES + 2,)), dma((GROUPS // LEVELS + 1,)), dma((GROUPS,)),
+            dma((TILES + 2,)), dma((GROUPS // BATCH + 1,)), dma((GROUPS,)),
             dma((GROUPS, 2)), dma((TILES + 1,)), dma((2,)), dma((2,)), dma((4,)), pltpu.SemaphoreType.REGULAR,
         ],
         compiler_params=pltpu.CompilerParams(has_side_effects=True, collective_id=0, vmem_limit_bytes=58 * 1024 * 1024),

time: 51.5 us -> 50.5 us (0.981)
  Pallas kernels: 50.4 us -> 49.5 us
    pallas_call x1, Pallas kernels: 50.4 us -> 49.5 us  [shards(): pl.pallas_call(kernel, out_shape=pltpu.VMEM(adjoint_guess.shape, F32), in...]
where the time goes in v4:
time: 50.5 us; the launch traced here: 50.4 us
  Pallas kernels  49.5 us (98%)
  local copies, waits for them, and re-layouts  0.97 us (2%)
    pallas_call x1, Pallas kernels, shards(): pl.pallas_call(kernel, out_shape=pltpu.VMEM(adjoint_guess.shape, F32), in...  49.5 us

profile of v4, /device:TPU:1, one launch (start us, length us, event | category | flops | bytes accessed | tf_op | source)
XLA Modules:
  0.0 50.4 jit_solution(4605602223664292122)
XLA Ops:
  0.0 49.5 %shard_map.46 = f32[8,2,32,512]{3,2,1,0:T(8,128)S(1)} custom-call(s32[32]{0:T(128)} %c_hbm.1, f32[8,2,32,512]{3,2,1,0:T(8,128)} %guess_hbm.1, f32[8,2,32,512]{3,2,1,0:T(8,128)} %src_hbm.1, bf16[8,2,32,512]{3,2,1,0:T(8,128)(2,1)} %vel_hbm.1), custom_call_target="tpu_custom_call" | custom-call | tf_op jit(solution)/shard_map/pallas_call | solution.py:559
  49.5 1.0 %copy.6 = f32[8,2,32,512]{3,2,1,0:T(8,128)} copy(f32[8,2,32,512]{3,2,1,0:T(8,128)S(1)} %shard_map.46) | data formatting | bytes 2097152

commit v5 on v4

--- a/solution.py
+++ b/solution.py
@@ -1,3 +1,5 @@
+import functools
+
 import jax
 import jax.numpy as jnp
 from jax import lax
@@ -451,31 +453,35 @@
             lax.fori_loop(low, high, coarse_coefficients, 0)
 
         prepare(GROUPS - LEVELS, GROUPS)
-
-        def solve(top):
+        prepare(0, GROUPS - LEVELS)
+
+        def decode(last_level):
+            arrived(rbuf.at[pl.ds(last_level, BATCH)], r_r.at[last_level // BATCH])
+            for n in range(BATCH):
+                level = last_level + n
+                whole = rbuf[level].astype(jnp.int32).astype(F32)
+                unit = jnp.exp2(0.125 * jnp.broadcast_to(whole[:, 0:1], whole.shape)) * (1.0 / WHOLE)
+                dec[level] = whole * unit * keep
+
+            @pl.when(is_end)
+            def _():
+                for n in range(BATCH):
+                    level = last_level + n
+                    arrived(xbuf.at[level], r_rx.at[level])
+                    dec[level] = jnp.where(from_extra, unfold(xbuf[level]) * keep, dec[level])
+
+        def solve(top, arriving):
             def several(turn, error):
                 first_level = top - BATCH * turn
-                last_level = first_level - BATCH + 1
-                arrived(rbuf.at[pl.ds(last_level, BATCH)], r_r.at[last_level // BATCH])
-                for n in range(BATCH):
-                    whole = rbuf[first_level - n].astype(jnp.int32).astype(F32)
-                    unit = jnp.exp2(0.125 * jnp.broadcast_to(whole[:, 0:1], whole.shape)) * (1.0 / WHOLE)
-                    dec[n] = whole * unit * keep
-
-                @pl.when(is_end)
-                def _():
-                    for n in range(BATCH):
-                        level = first_level - n
-                        arrived(xbuf.at[level], r_rx.at[level])
-                        dec[n] = jnp.where(from_extra, unfold(xbuf[level]) * keep, dec[n])
-
+                if arriving:
+                    decode(first_level - BATCH + 1)
                 for n in range(BATCH):
                     level = first_level - n
                     c = [coef[level, i] for i in range(6)]
                     new = c[0] * error + c[1] * roll(error, 64, 1)
                     new = new + (c[2] * roll(error, -1, 0) + c[3] * roll(error, 1, 0))
                     new = new + (c[4] * roll(error, -1, 1) + c[5] * roll(error, 1, 1))
-                    error = new + dec[n]
+                    error = new + dec[level]
                     for core in range(2):
                         low = new[ROWS * core : ROWS * core + ROWS // 2]
                         high = new[ROWS * core + ROWS // 2 : ROWS * (core + 1)]
@@ -488,16 +494,21 @@
 
             return several
 
-        error = lax.fori_loop(0, LEVELS // BATCH, solve(GROUPS - 1), jnp.zeros((2 * ROWS, 128), F32))
+        error = lax.fori_loop(0, LEVELS // BATCH, solve(GROUPS - 1, True), jnp.zeros((2 * ROWS, 128), F32))
         mine[...] = error
         for copy in refresh:
             copy.start()
-        prepare(0, GROUPS - LEVELS)
+
+        def decode_rest(turn, _):
+            decode(BATCH * turn)
+            return 0
+
+        lax.fori_loop(0, (GROUPS - LEVELS) // BATCH, decode_rest, 0)
         for copy in refresh:
             copy.wait_recv()
         error = jnp.where(place < REACH, roll(nbr[0], -32, 1), error)
         error = jnp.where(place >= 64 - REACH, roll(nbr[1], 32, 1), error) * keep
-        lax.fori_loop(0, LEVELS // BATCH, solve(GROUPS - LEVELS - 1), error)
+        lax.fori_loop(0, LEVELS // BATCH, solve(GROUPS - LEVELS - 1, False), error)
 
     for copy in relays:
         copy.wait_send()
@@ -512,33 +523,27 @@
         unused_windows(vbuf, lambda g: r_v.at[g // LEVELS])
         unused_windows(rbuf, lambda g: r_r.at[g // BATCH])
 
-    def wait_boxes(index, _):
-        pl.when(jnp.logical_not(is_owner & (index == tile)))(lambda: arrived(ebox.at[index], r_e.at[index]))
-        return 0
-
-    lax.fori_loop(0, TILES, wait_boxes, 0)
-
-    @pl.when((sx == 1) & owner_chip)
-    def _():
-        arrived(ebox.at[TILES], r_e.at[TILES])
-
     lane = iota((ROWS // 2, 128), 1)
-    for part in range(2):
-        rows = slice(part * ROWS // 2, (part + 1) * ROWS // 2)
-        for k in range(2):
-            for lane_tile in range(4):
+    for lane_tile in (0, 3, 1, 2):
+        lanes = slice(128 * lane_tile, 128 * lane_tile + 128)
+        for index in range(4 * lane_tile, 4 * lane_tile + 4):
+            pl.when(jnp.logical_not(is_owner & (index == tile)))(
+                functools.partial(arrived, ebox.at[index], r_e.at[index])
+            )
+        for part in range(2):
+            rows = slice(part * ROWS // 2, (part + 1) * ROWS // 2)
+            for k in range(2):
                 whole = None
                 for i in range(4):
                     piece = roll(ebox[4 * lane_tile + i], 32 * i - REACH - 64 * k - 32 * part, 1)
                     whole = piece if whole is None else jnp.where(lane >= 32 * i, piece, whole)
-                lanes = slice(128 * lane_tile, 128 * lane_tile + 128)
-                upd[k, rows, lanes] = upd[k, rows, lanes] + whole
-
-    def place_coarse(j, _):
-        out[j] = jnp.where(j == here, upd[...], out[j])
-        return 0
-
-    lax.fori_loop(0, STEPS, place_coarse, 0)
+                whole = upd[k, rows, lanes] + whole
+                for j in range(STEPS):
+                    out[j, k, rows, lanes] = jnp.where(here == j, whole, out[j, k, rows, lanes])
+
+    @pl.when((sx == 1) & owner_chip)
+    def _():
+        arrived(ebox.at[TILES], r_e.at[TILES])
 
     @pl.when(is_owner)
     def _():
@@ -591,7 +596,7 @@
             pltpu.VMEM((GROUPS + 1, 2 * ROWS, 128), jnp.bfloat16),
             pltpu.VMEM((GROUPS, 2 * EDGE, 128), F32),
             pltpu.VMEM((GROUPS, 6, 2 * ROWS, 128), F32),
-            pltpu.VMEM((BATCH, 2 * ROWS, 128), F32),
+            pltpu.VMEM((GROUPS, 2 * ROWS, 128), F32),
             pltpu.VMEM((GROUPS, 2, ROWS // 2, 128), F32),
             pltpu.VMEM((TILES + 1, ROWS // 2, 128), F32),
             pltpu.VMEM((2 * ROWS, 128), F32),

time: 50.5 us -> 49.8 us (0.986)
  Pallas kernels: 49.5 us -> 48.7 us
    pallas_call x1, Pallas kernels: 49.5 us -> 48.7 us  [shards(): pl.pallas_call(kernel, out_shape=pltpu.VMEM(adjoint_guess.shape, F32), in...]
where the time goes in v5:
time: 49.8 us; the launch traced here: 49.7 us
  Pallas kernels  48.7 us (98%)
  local copies, waits for them, and re-layouts  0.97 us (2%)
    pallas_call x1, Pallas kernels, shards(): pl.pallas_call(kernel, out_shape=pltpu.VMEM(adjoint_guess.shape, F32), in...  48.7 us

profile of v5, /device:TPU:1, one launch (start us, length us, event | category | flops | bytes accessed | tf_op | source)
XLA Modules:
  0.0 49.7 jit_solution(5741346359635621256)
XLA Ops:
  0.0 48.7 %shard_map.46 = f32[8,2,32,512]{3,2,1,0:T(8,128)S(1)} custom-call(s32[32]{0:T(128)} %c_hbm.1, f32[8,2,32,512]{3,2,1,0:T(8,128)} %guess_hbm.1, f32[8,2,32,512]{3,2,1,0:T(8,128)} %src_hbm.1, bf16[8,2,32,512]{3,2,1,0:T(8,128)(2,1)} %vel_hbm.1), custom_call_target="tpu_custom_call" | custom-call | tf_op jit(solution)/shard_map/pallas_call | solution.py:564
  48.7 1.0 %copy.6 = f32[8,2,32,512]{3,2,1,0:T(8,128)} copy(f32[8,2,32,512]{3,2,1,0:T(8,128)S(1)} %shard_map.46) | data formatting | bytes 2097152
